TPU v7x, 32 devices: a whole 2x2x4 slice. The times are simulated.
32 devices in a mesh: rep: 4 (over z), fsdp: 4 (over y, x), seq: 2 (over core).
Axes of the slice: x: 2, y: 2, z: 4, core: 2. Of those that a mesh axis runs over, the one named last changes fastest.
Arguments:
- tokens: bfloat16 [2, 16, 1024, 768], P(None, ('rep', 'fsdp'), 'seq'), may hold values from -6 to 6
- cotangent: bfloat16 [2, 16, 1024, 768], P(None, ('rep', 'fsdp'), 'seq'), may hold values from -6 to 6
- segments: int32 [2, 16, 1024], P(None, ('rep', 'fsdp')), may hold values from 0 to 3, as said below
- input_weight: float32 [768, 3328], P(('fsdp', 'seq')), may hold values from -0.21875 to 0.21875
- output_weight: float32 [1536, 768], P(('fsdp', 'seq')), may hold values from -0.15625 to 0.15625
- small_values: float32 [29768], replicated, may hold values from -12 to 2, as said below
- input_momentum: float32 [768, 3328], P(('fsdp', 'seq')), may hold values from -160 to 160
- output_momentum: float32 [1536, 768], P(('fsdp', 'seq')), may hold values from -160 to 160
- small_momentum: float32 [29768], replicated, may hold values from -16 to 16
- input_error: float32 [4, 768, 3328], P('rep', ('fsdp', 'seq')), may hold values from -1357.645 to 1357.645
- output_error: float32 [4, 1536, 768], P('rep', ('fsdp', 'seq')), may hold values from -1357.645 to 1357.645
- input_start: float32 [3328, 8], replicated, may hold values from -6 to 6
- output_start: float32 [768, 8], replicated, may hold values from -6 to 6
Outputs:
- output: bfloat16 [2, 16, 1024, 768], P(None, ('rep', 'fsdp'), 'seq')
- input_grad: bfloat16 [2, 16, 1024, 768], P(None, ('rep', 'fsdp'), 'seq')
- new_input_weight: float32 [768, 3328], P(('fsdp', 'seq'))
- new_output_weight: float32 [1536, 768], P(('fsdp', 'seq'))
- new_input_momentum: float32 [768, 3328], P(('fsdp', 'seq'))
- new_output_momentum: float32 [1536, 768], P(('fsdp', 'seq'))
- new_small_values: float32 [29768], replicated
- new_small_momentum: float32 [29768], replicated
- input_left: float32 [768, 8], P(('fsdp', 'seq'))
- input_right: float32 [3328, 8], replicated
- output_left: float32 [1536, 8], P(('fsdp', 'seq'))
- output_right: float32 [768, 8], replicated
- new_input_error: float32 [4, 768, 3328], P('rep', ('fsdp', 'seq'))
- new_output_error: float32 [4, 1536, 768], P('rep', ('fsdp', 'seq'))
Inputs may be any that keep to these rules, and one draw needn't show every extreme that they name: `segments`: within each sequence the ids never fall and run from 0 to 3: every sequence holds exactly 4 documents of 1 to 512 tokens, one of them exactly 512 tokens. `small_values`: the small parameters lie within this range.
All inputs are finite; a program needn't handle non-finite values.
Results may differ from a plain program's by a relative error of at most 0.012.
Values may be sent and summed in bfloat16 or wider, within the bound.
A program may use at most 192 MiB of HBM per device.

v0:
```python
from functools import partial
import math

import jax
import jax.numpy as jnp
from jax import lax
from jax.sharding import PartitionSpec as P

D = 768
INNER = 1536
HEADS = 24
HEADDIM = 64
STATE = 128
CONV = 4
GROUP = 256
PROJ = 3328
XBC = 1792


EPS = 1e-05
MOMENTUM = 0.9
HIGH = lax.Precision.HIGHEST


def from_behind(block, axis, distance):
    devices = range(lax.axis_size(axis))
    route = [(i - distance, i) for i in devices if i - distance in devices]
    return lax.ppermute(block, axis, route)


def entering(array, axis, combine, identity, reverse):
    count, place = (lax.axis_size(axis), lax.axis_index(axis))
    everything = jax.tree.map(
        lambda part, kind: lax.all_gather(part.astype(kind), axis),
        array,
        jax.tree.map(lambda a: jnp.bfloat16 if a.dtype == jnp.float32 else a.dtype, array),
    )
    start = jax.tree.map(
        lambda part, zero: jnp.broadcast_to(jnp.asarray(zero, part.dtype), part.shape),
        array,
        identity,
    )

    def step(k, before):
        at = count - 1 - k if reverse else k
        reached = at > place if reverse else at < place
        new = combine(
            before, jax.tree.map(lambda part, own: part[at].astype(own.dtype), everything, array)
        )
        return jax.tree.map(lambda a, b: jnp.where(reached, a, b), new, before)

    return lax.fori_loop(0, count, step, start)


def split_small(small_values):
    pieces = []
    offset = 0
    for amount in (D, D * HEADS, CONV * XBC, XBC, INNER, HEADS, HEADS, HEADS):
        pieces.append(small_values[offset : offset + amount])
        offset = offset + amount
    return (
        pieces[0],
        pieces[1].reshape(D, HEADS),
        pieces[2].reshape(CONV, XBC),
        pieces[3],
        pieces[4],
        pieces[5],
        pieces[6],
        pieces[7],
    )


def rms_scale(values, weights):
    return values * lax.rsqrt(jnp.mean(values * values, axis=-1, keepdims=True) + EPS) * weights


def step_rates(tokens_replica):
    grad_scale = 0.3 * math.sqrt(tokens_replica)
    return (
        0.5 / (math.sqrt(D) * grad_scale),
        0.5 / (math.sqrt(INNER) * grad_scale),
        0.1 / grad_scale,
    )


def convolve(documents, halo_documents, raw_rows, halo_rows, conv_weight, conv_bias):
    extended = jnp.concatenate([halo_rows, raw_rows], axis=0)
    wider_segments = jnp.concatenate([halo_documents, documents])
    extent = documents.shape[0]
    summed = jnp.zeros(raw_rows.shape, jnp.float32) + conv_bias[None, :]
    for offset in range(CONV):
        same_doc = jnp.where(wider_segments[offset : offset + extent] == documents, 1.0, 0.0)
        summed = (
            summed
            + conv_weight[offset][None, :] * extended[offset : offset + extent] * same_doc[:, None]
        )
    return jax.nn.silu(summed)


def group_output(
    value_block,
    write_block,
    read_block,
    delta_block,
    decay_block,
    segment_block,
    before,
    carried,
    skip_gain,
):
    extent = segment_block.shape[0]
    totals = jnp.cumsum(decay_block, axis=0)
    row_index = lax.broadcasted_iota(jnp.int32, (extent, extent), 0)
    col_index = lax.broadcasted_iota(jnp.int32, (extent, extent), 1)
    allowed = ((segment_block[:, None] == segment_block[None, :]) & (row_index >= col_index))[
        :, :, None
    ]
    spread = totals[:, None, :] - totals[None, :, :]
    decay_matrix = jnp.where(allowed, jnp.exp(jnp.where(allowed, spread, 0.0)), 0.0)
    scores = jnp.dot(read_block, write_block.T, precision=HIGH)
    mixing = decay_matrix * scores[:, :, None] * delta_block[None, :, :]
    inside = jnp.einsum("tsh,shp->thp", mixing, value_block, precision=HIGH)
    linked = jnp.where(segment_block == before, 1.0, 0.0)
    reading = jnp.einsum("tn,hpn->thp", read_block, carried, precision=HIGH)
    fading = jnp.exp(totals) * linked[:, None]
    return inside + fading[:, :, None] * reading + skip_gain[None, :, None] * value_block


def group_state(value_block, write_block, delta_block, decay_block, segment_block, before):
    totals = jnp.cumsum(decay_block, axis=0)
    keeping = jnp.where(segment_block == segment_block[-1], 1.0, 0.0)
    to_end = jnp.exp(totals[-1][None, :] - totals) * keeping[:, None] * delta_block
    fresh_state = jnp.einsum(
        "shp,sn->hpn", value_block * to_end[:, :, None], write_block, precision=HIGH
    )
    passing = jnp.exp(totals[-1]) * jnp.where(segment_block[-1] == before, 1.0, 0.0)
    return (fresh_state, passing)


def block_befores(documents, first_before):
    blocks = documents.shape[0] // GROUP
    segment_blocks = documents.reshape(blocks, GROUP)
    befores = jnp.concatenate(
        [
            jnp.reshape(first_before, (1,)).astype(jnp.int32),
            segment_blocks[:-1, -1].astype(jnp.int32),
        ]
    )
    return (blocks, segment_blocks, befores)


def run_states(documents, first_before, values, writers, deltas, log_decay):
    blocks, segment_blocks, befores = block_befores(documents, first_before)
    current_all = (
        values.reshape(blocks, GROUP, HEADS, HEADDIM),
        writers.reshape(blocks, GROUP, STATE),
        deltas.reshape(blocks, GROUP, HEADS),
        log_decay.reshape(blocks, GROUP, HEADS),
        segment_blocks,
        befores,
    )

    def advance(carried, current):
        state_now, passed = carried
        value_block, write_block, delta_block, decay_block, segment_block, before = current
        fresh_state, passing = group_state(
            value_block, write_block, delta_block, decay_block, segment_block, before
        )
        return (
            (passing[:, None, None] * state_now + fresh_state, passed * passing),
            (state_now, passed),
        )

    beginning = (jnp.zeros((HEADS, HEADDIM, STATE), jnp.float32), jnp.ones((HEADS,), jnp.float32))
    (final_state, final_pass), (block_starts, block_passes) = lax.scan(
        jax.checkpoint(advance), beginning, current_all
    )
    return (block_starts, block_passes, final_state, final_pass)


def run_outputs(
    documents,
    first_before,
    values,
    writers,
    readers,
    deltas,
    log_decay,
    block_starts,
    block_passes,
    incoming,
    skip_gain,
):
    blocks, segment_blocks, befores = block_befores(documents, first_before)
    current_all = (
        values.reshape(blocks, GROUP, HEADS, HEADDIM),
        writers.reshape(blocks, GROUP, STATE),
        readers.reshape(blocks, GROUP, STATE),
        deltas.reshape(blocks, GROUP, HEADS),
        log_decay.reshape(blocks, GROUP, HEADS),
        segment_blocks,
        befores,
        block_starts,
        block_passes,
    )

    def advance(nothing, current):
        (
            value_block,
            write_block,
            read_block,
            delta_block,
            decay_block,
            segment_block,
            before,
            start_state,
            passed,
        ) = current
        carried = start_state + passed[:, None, None] * incoming
        produced = group_output(
            value_block,
            write_block,
            read_block,
            delta_block,
            decay_block,
            segment_block,
            before,
            carried,
            skip_gain,
        )
        return (nothing, produced)

    unused, produced = lax.scan(jax.checkpoint(advance), jnp.zeros((), jnp.float32), current_all)
    return produced.reshape(documents.shape[0], HEADS, HEADDIM)


def chain_states(earlier, later):
    return (earlier[0] * later[0], later[0][:, :, None, None] * earlier[1] + later[1])


def delta_terms(delta_raw, dt_bias, log_rate):
    deltas = jax.nn.softplus(delta_raw + dt_bias)
    return (deltas, deltas * -jnp.exp(log_rate))


def gated_norm(mixed_rows, gate_rows, gate_gain):
    return rms_scale(mixed_rows * jax.nn.silu(gate_rows), gate_gain)


def orthonormal_from(factor, gram):
    lower = jnp.linalg.cholesky(gram)
    return lax.linalg.triangular_solve(lower, factor, left_side=False, lower=True, transpose_a=True)


def body(
    tokens,
    cotangent,
    segments,
    input_weight,
    output_weight,
    small_values,
    input_momentum,
    output_momentum,
    small_momentum,
    input_error,
    output_error,
    input_start,
    output_start,
):
    micro_count = tokens.shape[0]
    local_batch = tokens.shape[1]
    piece_length = tokens.shape[2]
    replicas = lax.axis_size("rep")
    tokens_replica = (
        micro_count * local_batch * piece_length * lax.axis_size("fsdp") * lax.axis_size("seq")
    )
    rate_in, rate_out, rate_small = step_rates(tokens_replica)
    begin = lax.axis_index("seq") * piece_length
    padded_segments = jnp.pad(segments, ((0, 0), (0, 0), (CONV - 1, 0)), constant_values=-1)
    wider_segments = lax.dynamic_slice_in_dim(padded_segments, begin, piece_length + CONV - 1, 2)
    own_segments = wider_segments[:, :, CONV - 1 :]
    norm_gain, delta_weight, conv_weight, conv_bias, gate_gain, dt_bias, log_rate, skip_gain = (
        split_small(small_values)
    )
    delta_low = delta_weight.astype(jnp.bfloat16)
    input_low = input_weight.astype(jnp.bfloat16)
    output_low = output_weight.astype(jnp.bfloat16)
    input_full = jnp.zeros((D, PROJ), jnp.float32)
    output_full = jnp.zeros((INNER, D), jnp.float32)
    small_total = jnp.zeros(small_values.shape, jnp.float32)
    conv_apply = jax.vmap(convolve, in_axes=(0, 0, 0, 0, None, None))
    states_apply = jax.vmap(run_states)
    outputs_apply = jax.vmap(run_outputs, in_axes=(0, 0, 0, 0, 0, 0, 0, 0, 0, 0, None))
    outputs = []
    input_grads = []
    for micro_step in range(micro_count):
        full_input, full_output = (
            lax.all_gather(input_low, ("fsdp", "seq"), axis=0, tiled=True),
            lax.all_gather(output_low, ("fsdp", "seq"), axis=0, tiled=True),
        )
        rows_in = tokens[micro_step].astype(jnp.float32)
        segment_rows = own_segments[micro_step]
        wider_rows = wider_segments[micro_step]
        first_before = wider_rows[:, CONV - 2]
        normed_in32, pre_back = jax.vjp(rms_scale, rows_in, norm_gain)
        normed_in = normed_in32.astype(jnp.bfloat16)
        projected = jnp.einsum(
            "bld,dk->blk", normed_in, full_input, preferred_element_type=jnp.float32
        ).astype(jnp.bfloat16)
        delta_raw = jnp.einsum(
            "bld,dh->blh", normed_in, delta_low, preferred_element_type=jnp.float32
        )
        gate_rows = projected[:, :, :INNER]
        raw_rows = projected[:, :, INNER:]
        halo_rows = from_behind(raw_rows[:, piece_length - (CONV - 1) :, :], "seq", 1)
        activated32, conv_back = jax.vjp(
            partial(conv_apply, segment_rows, wider_rows[:, : CONV - 1]),
            raw_rows.astype(jnp.float32),
            halo_rows.astype(jnp.float32),
            conv_weight,
            conv_bias,
        )
        activated = lax.optimization_barrier(activated32.astype(jnp.bfloat16)).astype(jnp.float32)
        values = activated[:, :, :INNER].reshape(local_batch, piece_length, HEADS, HEADDIM)
        writers = activated[:, :, INNER : INNER + STATE]
        readers = activated[:, :, INNER + STATE :]
        (deltas, log_decay), delta_back = jax.vjp(delta_terms, delta_raw, dt_bias, log_rate)
        (block_starts, block_passes, local_state, local_pass), states_back = jax.vjp(
            partial(states_apply, segment_rows, first_before), values, writers, deltas, log_decay
        )
        identity = (jnp.ones_like(local_pass), jnp.zeros_like(local_state))
        incoming = entering((local_pass, local_state), "seq", chain_states, identity, False)[1]
        mixed, outputs_back = jax.vjp(
            partial(outputs_apply, segment_rows, first_before),
            values,
            writers,
            readers,
            deltas,
            log_decay,
            block_starts,
            block_passes,
            incoming,
            skip_gain,
        )
        normed_out32, post_back = jax.vjp(
            gated_norm,
            mixed.reshape(local_batch, piece_length, INNER),
            gate_rows.astype(jnp.float32),
            gate_gain,
        )
        normed_out = normed_out32.astype(jnp.bfloat16)
        branch = jnp.einsum(
            "blk,kd->bld", normed_out, full_output, preferred_element_type=jnp.float32
        )
        outputs.append((rows_in + branch).astype(jnp.bfloat16))
        coming = cotangent[micro_step]
        output_part = jnp.einsum(
            "blk,bld->kd", normed_out, coming, preferred_element_type=jnp.float32
        )
        normed_grad = jnp.einsum(
            "bld,kd->blk", coming, full_output, preferred_element_type=jnp.float32
        )
        mixed_grad, gate_grad, gate_gain_grad = post_back(normed_grad)
        (
            value_one,
            writer_one,
            reader_grad,
            delta_one,
            decay_one,
            starts_grad,
            passes_grad,
            incoming_grad,
            skip_grad,
        ) = outputs_back(mixed_grad.reshape(local_batch, piece_length, HEADS, HEADDIM))
        outgoing_grad = entering((local_pass, incoming_grad), "seq", chain_states, identity, True)[
            1
        ]
        pass_grad = jnp.sum(outgoing_grad * incoming, axis=(2, 3))
        value_two, writer_two, delta_two, decay_two = states_back(
            (starts_grad, passes_grad, outgoing_grad, pass_grad)
        )
        delta_grad, bias_grad, rate_grad = delta_back(
            (delta_one + delta_two, decay_one + decay_two)
        )
        activated_grad = jnp.concatenate(
            [
                (value_one + value_two).reshape(local_batch, piece_length, INNER),
                writer_one + writer_two,
                reader_grad,
            ],
            axis=2,
        )
        raw_grad, halo_grad, conv_weight_grad, conv_bias_grad = conv_back(activated_grad)
        returned = from_behind(halo_grad, "seq", -1)
        raw_grad = jnp.concatenate(
            [
                raw_grad[:, : piece_length - (CONV - 1)],
                raw_grad[:, piece_length - (CONV - 1) :] + returned,
            ],
            axis=1,
        )
        projected_grad = jnp.concatenate([gate_grad, raw_grad], axis=2).astype(jnp.bfloat16)
        delta_grad_low = delta_grad.astype(jnp.bfloat16)
        input_part = jnp.einsum(
            "bld,blk->dk", normed_in, projected_grad, preferred_element_type=jnp.float32
        )
        delta_weight_grad = jnp.einsum(
            "bld,blh->dh", normed_in, delta_grad_low, preferred_element_type=jnp.float32
        )
        normed_in_grad = jnp.einsum(
            "blk,dk->bld", projected_grad, full_input, preferred_element_type=jnp.float32
        ) + jnp.einsum("blh,dh->bld", delta_grad_low, delta_low, preferred_element_type=jnp.float32)
        rows_grad, norm_gain_grad = pre_back(normed_in_grad)
        input_grads.append((coming.astype(jnp.float32) + rows_grad).astype(jnp.bfloat16))
        small_total = small_total + jnp.concatenate(
            [
                norm_gain_grad,
                delta_weight_grad.reshape(-1),
                conv_weight_grad.reshape(-1),
                conv_bias_grad,
                gate_gain_grad,
                bias_grad,
                rate_grad,
                skip_grad,
            ]
        )
        input_full = input_full + input_part
        output_full = output_full + output_part
    input_total, output_total = (
        lax.psum_scatter(
            input_full.astype(jnp.bfloat16), ("fsdp", "seq"), scatter_dimension=0, tiled=True
        ).astype(jnp.float32),
        lax.psum_scatter(
            output_full.astype(jnp.bfloat16), ("fsdp", "seq"), scatter_dimension=0, tiled=True
        ).astype(jnp.float32),
    )
    input_mixed = input_total + input_error[0]
    output_mixed = output_total + output_error[0]
    left_in, left_out = lax.psum(
        (
            jnp.dot(input_mixed, input_start, precision=HIGH),
            jnp.dot(output_mixed, output_start, precision=HIGH),
        ),
        "rep",
    )
    left_in = left_in / replicas
    left_out = left_out / replicas
    gram_in, gram_out = lax.psum(
        (
            jnp.dot(left_in.T, left_in, precision=HIGH),
            jnp.dot(left_out.T, left_out, precision=HIGH),
        ),
        ("fsdp", "seq"),
    )
    input_left = orthonormal_from(left_in, gram_in)
    output_left = orthonormal_from(left_out, gram_out)
    right_in, right_out, small_sum = lax.psum(
        (
            jnp.dot(input_mixed.T, input_left, precision=HIGH),
            jnp.dot(output_mixed.T, output_left, precision=HIGH),
            small_total,
        ),
        ("rep", "fsdp", "seq"),
    )
    input_right = right_in / replicas
    output_right = right_out / replicas
    approx_in = jnp.dot(input_left, input_right.T, precision=HIGH)
    approx_out = jnp.dot(output_left, output_right.T, precision=HIGH)
    new_input_momentum = MOMENTUM * input_momentum + approx_in
    new_output_momentum = MOMENTUM * output_momentum + approx_out
    new_input_weight = input_weight - rate_in * new_input_momentum
    new_output_weight = output_weight - rate_out * new_output_momentum
    new_small_momentum = MOMENTUM * small_momentum + small_sum / replicas
    new_small_values = small_values - rate_small * new_small_momentum
    return (
        jnp.stack(outputs),
        jnp.stack(input_grads),
        new_input_weight,
        new_output_weight,
        new_input_momentum,
        new_output_momentum,
        new_small_values,
        new_small_momentum,
        input_left,
        input_right,
        output_left,
        output_right,
        (input_mixed - approx_in)[None],
        (output_mixed - approx_out)[None],
    )


def solution(mesh):
    return jax.shard_map(
        body,
        mesh=mesh,
        in_specs=(
            P(None, ("rep", "fsdp"), "seq", None),
            P(None, ("rep", "fsdp"), "seq", None),
            P(None, ("rep", "fsdp"), None),
            P(("fsdp", "seq"), None),
            P(("fsdp", "seq"), None),
            P(),
            P(("fsdp", "seq"), None),
            P(("fsdp", "seq"), None),
            P(),
            P("rep", ("fsdp", "seq"), None),
            P("rep", ("fsdp", "seq"), None),
            P(),
            P(),
        ),
        out_specs=(
            P(None, ("rep", "fsdp"), "seq", None),
            P(None, ("rep", "fsdp"), "seq", None),
            P(("fsdp", "seq"), None),
            P(("fsdp", "seq"), None),
            P(("fsdp", "seq"), None),
            P(("fsdp", "seq"), None),
            P(),
            P(),
            P(("fsdp", "seq"), None),
            P(),
            P(("fsdp", "seq"), None),
            P(),
            P("rep", ("fsdp", "seq"), None),
            P("rep", ("fsdp", "seq"), None),
        ),
        check_vma=False,
    )
```

profile of v0, /device:TPU:0, one launch (start us, length us, event | category | flops | bytes accessed | tf_op | source)
XLA Modules:
  0.0 1118.8 jit_solution(14426521297872455887)
XLA Ops:
  30.4 11.9 %all-gather.13.cloned.1.call-done = bf16[1536,768]{1,0:T(8,128)(2,1)} async-done(((bf16[192,768]{1,0:T(8,128)(2,1)}), bf16[1536,768]{1,0:T(8,128)(2,1)}) %all-gather.13.cloned.1.call-update) | async-done | bytes 2359312 | tf_op jit(solution)/shard_map/all_gather | solution.py:299
  47.3 38.1 %all-gather.11.cloned.1.call-done = bf16[768,3328]{1,0:T(8,128)(2,1)} async-done(((bf16[96,3328]{1,0:T(8,128)(2,1)}), bf16[768,3328]{1,0:T(8,128)(2,1)}) %all-gather.11.cloned.1.call-update) | async-done | bytes 5111824 | tf_op jit(solution)/shard_map/all_gather | solution.py:298
  122.6 23.3 %while.238 = (s32[]{:T(128)}, f32[1,24,64,128]{3,2,1,0:T(8,128)S(1)}, f32[1,24]{1,0:T(1,128)S(1)}, f32[2,1,24,64,128]{4,3,2,1,0:T(8,128)}, f32[2,1,24]{2,1,0:T(1...) while((s32[]{:T(128)}, ...), condition=%wide.region_4.6_spmd.clone, body=%wide.region_1.5_spmd.clone.sunk | while | flops 605964992 | bytes 5303248 | solution.py:175
  148.4 10.7 multiply_convert_fusion
  166.6 32.7 %while.236 = (s32[]{:T(128)}, f32[2,1,256,24,64]{2,4,3,1,0:T(8,128)}, f32[2,1,256,24,64]{2,4,3,1,0:T(8,128)}, s32[2,1,256]{2,1,0:T(1,128)S(1)}, f32[2,1,256,24]{...) while((s32[]{:T(128)}, ...), condition=%wide.region_10.12_spmd.clone, body=%wide.region_7.11_spmd.clone.sunk | while | flops 1923422720 | bytes 23646384 | solution.py:233
  174.3 8.6 fusion.605
  190.7 8.6 fusion.605
  229.8 31.3 %while.240 = (s32[]{:T(128)}, f32[1,24,64,128]{3,2,1,0:T(8,128)}, f32[1,24]{1,0:T(1,128)}, f32[2,1,24,64,128]{4,3,2,1,0:T(8,128)S(1)}, f32[2,1,24]{2,1,0:T(1,128...) while((s32[]{:T(128)}, f32[1,24,64,128]{3,2,1,0:T(8,128)}, ...), condition=%wide.region_16.18_spmd.clone, body=%wide.region_13.17_spmd.clone.sunk | while | flops 605964992 | bytes 5303564 | solution.py:175
  271.9 39.9 %while.237 = (s32[]{:T(128)}, f32[2,1,256,24,64]{2,4,3,1,0:T(8,128)}, f32[2,1,256,24,64]{2,4,3,1,0:T(8,128)}, s32[2,1,256]{2,1,0:T(1,128)S(1)}, f32[2,1,256,24]{...) while((s32[]{:T(128)}, ...), condition=%wide.region_22.24_spmd.clone, body=%wide.region_19.23_spmd.clone.sunk | while | flops 1923422720 | bytes 24900284 | solution.py:233
  283.2 8.6 fusion.616
  303.2 8.6 fusion.616
  333.4 7.4 fusion.301
  343.0 8.2 fusion.342
  369.6 114.9 %while.242 = (s32[]{:T(128)}, f32[1,24,64,128]{3,2,1,0:T(8,128)}, f32[24]{0:T(128)}, f32[2,1,256,24,64]{2,4,3,1,0:T(8,128)}, f32[2,1,256,128]{3,2,1,0:T(8,128)},...) while((s32[]{:T(128)}, f32[1,24,64,128]{3,2,1,0:T(8,128)}, ...), condition=%wide.region_37.39_spmd.clone, body=%wide.region_25.38_spmd.clone.sunk | while | flops 4567970304 | bytes 68344960 | solution.py:233
  388.4 12.3 %fusion.646 = (f32[256,24]{0,1:T(8,128)S(1)}, f32[256,24]{0,1:T(8,128)S(1)}, f32[256,24]{0,1:T(8,128)}, f32[256,256]{1,0:T(8,128)}) fusion(f32[256,256]{1,0:T(8,128)} %fusion.643, f32[256,24]{0,1:T(8,128)} %bitcast.1713, f32[256,24]{0,1:T(8,128)S(1)} %bitcast.1717, pred[256,256]{1,0:T(8,128)(4,1)S(1)} %fusion.644, ...), kind=kOutput, calls=%fused_computation.297.clone.1 | convolution fusion | flops 1231468544 | bytes 3858432 | tf_op jit(solution)/shard_map/transpose(jvp(vmap()))/while/body/eval_jaxpr/checkpoint/tsh,shp->thp/dot_general | solution.py:122
  415.0 7.5 fusion.645
  444.9 12.3 %fusion.646 = (f32[256,24]{0,1:T(8,128)S(1)}, f32[256,24]{0,1:T(8,128)S(1)}, f32[256,24]{0,1:T(8,128)}, f32[256,256]{1,0:T(8,128)}) fusion(f32[256,256]{1,0:T(8,128)} %fusion.643, f32[256,24]{0,1:T(8,128)} %bitcast.1713, f32[256,24]{0,1:T(8,128)S(1)} %bitcast.1717, pred[256,256]{1,0:T(8,128)(4,1)S(1)} %fusion.644, ...), kind=kOutput, calls=%fused_computation.297.clone.1 | convolution fusion | flops 1231468544 | bytes 3858432 | tf_op jit(solution)/shard_map/transpose(jvp(vmap()))/while/body/eval_jaxpr/checkpoint/tsh,shp->thp/dot_general | solution.py:122
  471.5 7.5 fusion.645
  494.8 62.4 %while.234 = (s32[]{:T(128)}, f32[1,24,64,128]{3,2,1,0:T(8,128)S(1)}, f32[1,24]{1,0:T(1,128)}, f32[2,1,256,24,64]{2,4,3,1,0:T(8,128)}, f32[2,1,256,128]{3,2,1,0:...) while((s32[]{:T(128)}, ...), condition=%wide.region_49.51_spmd, body=%wide.region_41.50_spmd.sunk | while | flops 1211954048 | bytes 40085732 | solution.py:175
  587.4 111.1 %while.244 = (s32[]{:T(128)}, f32[1,24,64,128]{3,2,1,0:T(8,128)}, f32[24]{0:T(128)}, f32[2,1,256,24,64]{2,4,3,1,0:T(8,128)}, f32[2,1,256,128]{3,2,1,0:T(8,128)},...) while((s32[]{:T(128)}, f32[1,24,64,128]{3,2,1,0:T(8,128)}, ...), condition=%wide.region_64.66_spmd.clone, body=%wide.region_52.65_spmd.clone.sunk | while | flops 4567970304 | bytes 74833088 | solution.py:233
  604.2 12.3 %fusion.671 = (f32[256,24]{0,1:T(8,128)S(1)}, f32[256,24]{0,1:T(8,128)S(1)}, f32[256,24]{0,1:T(8,128)}, f32[256,256]{1,0:T(8,128)}) fusion(f32[256,256]{1,0:T(8,128)} %fusion.668, f32[256,24]{0,1:T(8,128)} %bitcast.1715, f32[256,24]{0,1:T(8,128)S(1)} %bitcast.1719, pred[256,256]{1,0:T(8,128)(4,1)S(1)} %fusion.669, ...), kind=kOutput, calls=%fused_computation.387.clone.1 | convolution fusion | flops 1231468544 | bytes 3858432 | tf_op jit(solution)/shard_map/transpose(jvp(vmap()))/while/body/eval_jaxpr/checkpoint/tsh,shp->thp/dot_general | solution.py:122
  630.8 7.5 fusion.670
  658.8 12.3 %fusion.671 = (f32[256,24]{0,1:T(8,128)S(1)}, f32[256,24]{0,1:T(8,128)S(1)}, f32[256,24]{0,1:T(8,128)}, f32[256,256]{1,0:T(8,128)}) fusion(f32[256,256]{1,0:T(8,128)} %fusion.668, f32[256,24]{0,1:T(8,128)} %bitcast.1715, f32[256,24]{0,1:T(8,128)S(1)} %bitcast.1719, pred[256,256]{1,0:T(8,128)(4,1)S(1)} %fusion.669, ...), kind=kOutput, calls=%fused_computation.387.clone.1 | convolution fusion | flops 1231468544 | bytes 3858432 | tf_op jit(solution)/shard_map/transpose(jvp(vmap()))/while/body/eval_jaxpr/checkpoint/tsh,shp->thp/dot_general | solution.py:122
  685.4 7.5 fusion.670
  708.6 62.4 %while.235 = (s32[]{:T(128)}, f32[1,24,64,128]{3,2,1,0:T(8,128)S(1)}, f32[1,24]{1,0:T(1,128)}, f32[2,1,256,24,64]{2,4,3,1,0:T(8,128)}, f32[2,1,256,128]{3,2,1,0:...) while((s32[]{:T(128)}, ...), condition=%wide.region_76.78_spmd, body=%wide.region_68.77_spmd.sunk | while | flops 1211954048 | bytes 40085732 | solution.py:175
  787.3 12.4 %multiply_reduce_fusion.14 = (f32[1792]{0:T(1024)}, f32[1792]{0:T(1024)}, f32[1792]{0:T(1024)}, f32[1792]{0:T(1024)S(1)}, f32[1792]{0:T(1024)}, /*index=5*/f32[1,512,1792]{2,1,0:T(8,128)}) fusion(f32[1,512,1792]{2,1,0:T(8,128)} %copy-done.27, f32[1,3,1792]{2,1,0:T(4,128)S(1)} %copy-done.134, f32[512]{0:T(512)} %bitcast.1772, f32[512]{0:T(512)} %bitcast.1769, ...), kind=kLoop, calls=%fused_computation.506 | loop fusion | flops 24763648 | bytes 16578560 | tf_op jit(solution)/shard_map/transpose(jvp(vmap()))/reduce_sum | solution.py:95
  805.8 7.5 broadcast_multiply_fusion
  885.7 12.4 %reduce-scatter.3.cloned.1.call-done = bf16[96,3328]{1,0:T(8,128)(2,1)} async-done(((bf16[768,3328]{1,0:T(8,128)(2,1)}), bf16[96,3328]{1,0:T(8,128)(2,1)}) %reduce-scatter.3.cloned.1.call-update) | async-done | bytes 638992 | tf_op jit(solution)/shard_map/reduce_scatter | solution.py:430
  900.4 18.7 %all-reduce.23 = (f32[96,8]{0,1:T(8,128)S(1)}, f32[192,8]{0,1:T(8,128)S(1)}) all-reduce(f32[96,8]{0,1:T(8,128)S(1)} %fusion.367, f32[192,8]{0,1:T(8,128)S(1)} %fusion.369), channel_id=1, replica_groups=mesh['rep'=4,'fsdp'=4,'seq'=2] {'rep'}, use_global_device_ids=true, to_apply=%region_79.81 | all-reduce | flops 2304 | bytes 18432 | tf_op jit(solution)/shard_map/psum | solution.py:439
  919.4 12.6 %all-reduce.22 = (f32[8,8]{0,1:T(8,128)}, f32[8,8]{0,1:T(8,128)S(1)}) all-reduce(f32[8,8]{0,1:T(8,128)S(1)} %fusion.412, f32[8,8]{0,1:T(8,128)S(1)} %fusion.400), channel_id=1, replica_groups=mesh['rep'=4,'fsdp'=4,'seq'=2] {'fsdp','seq'}, use_global_device_ids=true, to_apply=%region_80.82 | all-reduce | flops 128 | bytes 1024 | tf_op jit(solution)/shard_map/psum | solution.py:448
  935.4 37.2 %psum.54 = f32[768,8]{0,1:T(8,128)S(1)} all-reduce(f32[768,8]{0,1:T(8,128)S(1)} %fusion.368), channel_id=1, replica_groups=mesh['rep'=4,'fsdp'=4,'seq'=2] {'rep','fsdp','seq'}, use_global_device_ids=true, to_apply=%region_87.90 | all-reduce | flops 6144 | bytes 49152 | tf_op jit(solution)/shard_map/psum | solution.py:457
  982.3 122.0 %all-reduce.26.cloned.1.call-done = (f32[3328,8]{0,1:T(8,128)}, f32[29768]{0:T(1024)}) async-done(((f32[3328,8]{0,1:T(8,128)}, f32[29768]{0:T(1024)}), (f32[3328,8]{0,1:T(8,128)}, f32[29768]{0:T(1024)})) %all-reduce.26.cloned.1.call-update) | async-done | bytes 225584 | tf_op jit(solution)/shard_map/psum | solution.py:457
  (1410 shorter events, 682.1 us)
Async XLA Ops:
  7.2 891.0 %copy-start = (f32[3328,8]{0,1:T(8,128)S(1)}, f32[3328,8]{0,1:T(8,128)}, u32[]{:S(2)}) copy-start(f32[3328,8]{0,1:T(8,128)} %param.50) | copy-start | bytes 319492
  7.2 35.0 %all-gather.13.cloned.1.call-start = ((), (), s32[]{:S(2)}) async-start(), calls=%async_computation.3 | async-start | bytes 2654208 | tf_op jit(solution)/shard_map/all_gather | solution.py:299
  9.1 76.2 %all-gather.11.cloned.1.call-start = ((), (), s32[]{:S(2)}) async-start(), calls=%async_computation.2 | async-start | bytes 5750784 | tf_op jit(solution)/shard_map/all_gather | solution.py:298
  11.4 872.7 %reduce-scatter.5.cloned.1.call-start = ((), (), s32[]{:S(2)}) async-start(), calls=%async_computation.5 | async-start | bytes 2654208 | tf_op jit(solution)/shard_map/reduce_scatter | solution.py:433
  12.2 82.8 %copy-start.121 = (f32[768]{0:T(1024)}, f32[768]{0:T(1024)S(1)}, u32[]{:S(2)}) copy-start(f32[768]{0:T(1024)S(1)} %slice.465) | copy-start | bytes 9220
  16.2 31.1 %copy-start.89 = (bf16[768,24]{1,0:T(8,128)(2,1)}, bf16[768,24]{1,0:T(8,128)(2,1)S(1)}, u32[]{:S(2)}) copy-start(bf16[768,24]{1,0:T(8,128)(2,1)S(1)} %convert_element_type.395) | copy-start | bytes 110596
  18.7 66.7 %copy-start.152 = (f32[512]{0:T(512)}, f32[512]{0:T(512)S(1)}, u32[]{:S(2)}) copy-start(f32[512]{0:T(512)S(1)} %get-tuple-element.4103) | copy-start | bytes 6148
  18.7 76.3 %copy-start.182 = (f32[512]{0:T(512)}, f32[512]{0:T(512)S(1)}, u32[]{:S(2)}) copy-start(f32[512]{0:T(512)S(1)} %get-tuple-element.4104) | copy-start | bytes 6148
  30.2 72.1 %copy-start.185 = (f32[1,512]{1,0:T(1,128)}, f32[1,512]{1,0:T(1,128)S(1)}, u32[]{:S(2)}) copy-start(f32[1,512]{1,0:T(1,128)S(1)} %get-tuple-element.4088) | copy-start | bytes 6148
  30.2 72.1 %copy-start.188 = (f32[1,512]{1,0:T(1,128)}, f32[1,512]{1,0:T(1,128)S(1)}, u32[]{:S(2)}) copy-start(f32[1,512]{1,0:T(1,128)S(1)} %get-tuple-element.4089) | copy-start | bytes 6148
  30.2 72.1 %copy-start.190 = (f32[1,512]{1,0:T(1,128)}, f32[1,512]{1,0:T(1,128)S(1)}, u32[]{:S(2)}) copy-start(f32[1,512]{1,0:T(1,128)S(1)} %get-tuple-element.4090) | copy-start | bytes 6148
  30.3 118.1 %copy-start.192 = (f32[1,512]{1,0:T(1,128)}, f32[1,512]{1,0:T(1,128)S(1)}, u32[]{:S(2)}) copy-start(f32[1,512]{1,0:T(1,128)S(1)} %get-tuple-element.4091) | copy-start | bytes 6148
  30.3 118.1 %copy-start.195 = (f32[1,512]{1,0:T(1,128)}, f32[1,512]{1,0:T(1,128)S(1)}, u32[]{:S(2)}) copy-start(f32[1,512]{1,0:T(1,128)S(1)} %get-tuple-element.4092) | copy-start | bytes 6148
  30.3 118.1 %copy-start.198 = (f32[1,512]{1,0:T(1,128)}, f32[1,512]{1,0:T(1,128)S(1)}, u32[]{:S(2)}) copy-start(f32[1,512]{1,0:T(1,128)S(1)} %get-tuple-element.4093) | copy-start | bytes 6148
  30.3 118.0 %copy-start.154 = (f32[1792]{0:T(1024)}, f32[1792]{0:T(1024)S(1)}, u32[]{:S(2)}) copy-start(f32[1792]{0:T(1024)S(1)} %get-tuple-element.4066) | copy-start | bytes 21508
  30.4 118.0 %copy-start.156 = (f32[1792]{0:T(1024)}, f32[1792]{0:T(1024)S(1)}, u32[]{:S(2)}) copy-start(f32[1792]{0:T(1024)S(1)} %get-tuple-element.4067) | copy-start | bytes 21508
  30.4 118.0 %copy-start.158 = (f32[1792]{0:T(1024)}, f32[1792]{0:T(1024)S(1)}, u32[]{:S(2)}) copy-start(f32[1792]{0:T(1024)S(1)} %get-tuple-element.4068) | copy-start | bytes 21508
  30.4 118.0 %copy-start.160 = (f32[1792]{0:T(1024)}, f32[1792]{0:T(1024)S(1)}, u32[]{:S(2)}) copy-start(f32[1792]{0:T(1024)S(1)} %get-tuple-element.4069) | copy-start | bytes 21508
  92.8 9.4 collective-permute-start
  100.6 47.7 %collective-permute-start.1 = (bf16[1,3,1792]{2,1,0:T(4,128)(2,1)S(1)}, bf16[1,3,1792]{2,1,0:T(4,128)(2,1)S(1)}, u32[]{:S(2)}, u32[]{:S(2)}) collective-permute-start(bf16[1,3,1792]{2,1,0:T(4,128)(2,1)S(1)} %slice.571), channel_id=1, source_target_pairs={{0,1},{2,3},{4,5},{6,7},{8,9},{10,11},{12,13},{14,15},{16,17},{18,... | collective-permute-start | bytes 32264 | tf_op jit(solution)/shard_map/ppermute | solution.py:28
  333.3 564.8 %reduce-scatter.3.cloned.1.call-start = ((), (), s32[]{:S(2)}) async-start(), calls=%async_computation.4 | async-start | bytes 5750784 | tf_op jit(solution)/shard_map/reduce_scatter | solution.py:430
  369.6 118.5 %copy-start.4 = (f32[1,24,64,128]{3,2,1,0:T(8,128)S(1)}, f32[1,24,64,128]{3,2,1,0:T(8,128)}, u32[]{:S(2)}) copy-start(f32[1,24,64,128]{3,2,1,0:T(8,128)} %custom-call.18) | copy-start | bytes 2359300
  587.4 114.7 %copy-start.3 = (f32[1,24,64,128]{3,2,1,0:T(8,128)S(1)}, f32[1,24,64,128]{3,2,1,0:T(8,128)}, u32[]{:S(2)}) copy-start(f32[1,24,64,128]{3,2,1,0:T(8,128)} %custom-call.21) | copy-start | bytes 2359300
  814.1 14.5 %collective-permute-start.2 = (f32[1,3,1792]{2,1,0:T(4,128)S(1)}, f32[1,3,1792]{2,1,0:T(4,128)S(1)}, u32[]{:S(2)}, u32[]{:S(2)}) collective-permute-start(f32[1,3,1792]{2,1,0:T(4,128)S(1)} %pad_add_fusion.5), channel_id=1, source_target_pairs={{1,0},{3,2},{5,4},{7,6},{9,8},{11,10},{13,12},{15,14},{17,16},{19,... | collective-permute-start | bytes 64520 | tf_op jit(solution)/shard_map/ppermute | solution.py:28
  827.0 3.5 collective-permute-start.3
  841.6 262.7 %all-reduce.26.cloned.1.call-start = ((), (), s32[]{:S(2)}) async-start(), calls=%async_computation.6 | async-start | bytes 458752 | tf_op jit(solution)/shard_map/psum | solution.py:457
  884.1 95.1 %copy-start.88 = (f32[192,768]{1,0:T(8,128)S(1)}, f32[192,768]{1,0:T(8,128)}, u32[]{:S(2)}) copy-start(f32[192,768]{1,0:T(8,128)} %param.43) | copy-start | bytes 1769476
  884.1 50.8 %copy-start.80 = (bf16[192,768]{1,0:T(8,128)(2,1)S(1)}, bf16[192,768]{1,0:T(8,128)(2,1)}, u32[]{:S(2)}) copy-start(bf16[192,768]{1,0:T(8,128)(2,1)} %reduce-scatter.5.cloned.1.call-done) | copy-start | bytes 884740
  898.1 79.5 %copy-start.76 = (bf16[96,3328]{1,0:T(8,128)(2,1)S(1)}, bf16[96,3328]{1,0:T(8,128)(2,1)}, u32[]{:S(2)}) copy-start(bf16[96,3328]{1,0:T(8,128)(2,1)} %reduce-scatter.3.cloned.1.call-done) | copy-start | bytes 1916932
  934.9 47.3 %copy-start.177 = (f32[192,8]{0,1:T(8,128)}, f32[192,8]{0,1:T(8,128)S(1)}, u32[]{:S(2)}) copy-start(f32[192,8]{0,1:T(8,128)S(1)} %fusion.398) | copy-start | bytes 18436
  972.6 132.5 %copy-start.168 = (f32[768,8]{0,1:T(8,128)}, f32[768,8]{0,1:T(8,128)S(1)}, u32[]{:S(2)}) copy-start(f32[768,8]{0,1:T(8,128)S(1)} %broadcast_multiply_fusion.5) | copy-start | bytes 73732
  977.7 129.3 %copy-start.217 = (f32[96,8]{0,1:T(8,128)}, f32[96,8]{0,1:T(8,128)S(1)}, u32[]{:S(2)}) copy-start(f32[96,8]{0,1:T(8,128)S(1)} %fusion.405) | copy-start | bytes 9220
  (300 other events, 1668.9 us)
Sparse Core Ops, SparseCore 0:
  10.5 31.7 all-gather.12
  44.7 40.5 all-gather.10
  333.4 42.4 reduce-scatter.4
  841.7 56.3 reduce-scatter.2
  979.3 124.9 all-reduce.25
where the time goes:
time: 1130 us; the launch traced here: 1120 us
  local copies, waits for them, and re-layouts  313 us (28%)
  matrix products  278 us (25%)
  other arithmetic  223 us (20%)
  waiting for transfers between devices  185 us (16%)
  blocking collectives  82.4 us (7%)
  between operations  15.9 us (1%)
  loops' own time  14.4 us (1%)
    psum x1, waiting for transfers between devices, body(): lax.psum((jnp.dot(input_mixed.T, input_left, precision=HIGH), jnp.dot(out...  122 us
    dot_general x12, matrix products, group_output(): inside = jnp.einsum('tsh,shp->thp', mixing, value_block, precision=HIGH)  114 us
    another operation x172, local copies, waits for them, and re-layouts  65.4 us
    dot_general x16, matrix products, group_output(): reading = jnp.einsum('tn,hpn->thp', read_block, carried, precision=HIGH)  45.7 us
    another operation x58, other arithmetic  41.6 us
    all_gather x1, waiting for transfers between devices, body(): lax.all_gather(input_low, ('fsdp', 'seq'), axis=0, tiled=True)  38.1 us
    psum x1, blocking collectives, body(): lax.psum((jnp.dot(input_mixed.T, input_left, precision=HIGH), jnp.dot(out...  37.2 us
    dot_general x12, matrix products, group_state(): jnp.einsum('shp,sn->hpn', value_block * to_end[:, :, None], write_block,...  36.6 us
  transfers between devices with their start and end apart: 9, of which 5 were waited for; matrix products, arithmetic and copies ran while one was open for 52% of the time, Pallas kernels for 0%

commit v1 on v0

v1 whole, which is shorter than its diff:
```python
from functools import partial
import math

import jax
import jax.numpy as jnp
from jax import lax
from jax.experimental import pallas as pl
from jax.experimental.pallas import tpu as pltpu
from jax.sharding import PartitionSpec as P

D = 768
INNER = 1536
HEADS = 24
HEADDIM = 64
STATE = 128
CONV = 4
PROJ = 3328
XBC = 1792

EPS = 1e-05
MOMENTUM = 0.9
HIGH = lax.Precision.HIGHEST
F32 = jnp.float32
BF16 = jnp.bfloat16
HP = 32
CH = 128
HALO = 16
TILE = 256
NEG = -1e30
VMEM_LIMIT = 58 * 2**20


def nn(a, b):
    return lax.dot_general(a, b, (((1,), (0,)), ((), ())), preferred_element_type=F32)


def nt(a, b):
    return lax.dot_general(a, b, (((1,), (1,)), ((), ())), preferred_element_type=F32)


def tn(a, b):
    return lax.dot_general(a, b, (((0,), (0,)), ((), ())), preferred_element_type=F32)


def nn_high(a, b):
    return lax.dot_general(
        a, b, (((1,), (0,)), ((), ())), precision=HIGH, preferred_element_type=F32
    )


def softplus(v):
    return jnp.maximum(v, 0.0) + jnp.log1p(jnp.exp(-jnp.abs(v)))


def triangle(extent):
    return jnp.where(
        lax.broadcasted_iota(jnp.int32, (extent, extent), 0)
        <= lax.broadcasted_iota(jnp.int32, (extent, extent), 1),
        1.0,
        0.0,
    )


def params(semantics, **more):
    return pltpu.CompilerParams(
        dimension_semantics=semantics, vmem_limit_bytes=VMEM_LIMIT, **more
    )


def enter_kernel(
    tok_ref, halo_ref, gain_ref, wraw_ref, dlow_ref, cw_ref, cb_ref, same_ref,
    bias_ref, rate_ref, segrow_ref,
    normed_ref, raw_ref, dsilu_ref, val_ref, wr_ref, draw_ref, delta_ref, send_ref,
    ext, rawbuf, act, mask, weight,
):
    length = tok_ref.shape[1]
    gain = gain_ref[...]
    for start, rows, src in ((0, HALO, halo_ref), (HALO, length, tok_ref)):
        for b in range(0, rows, 128):
            n = min(128, rows - b)
            x = src[0, b : b + n, :].astype(F32)
            scale = lax.rsqrt(jnp.mean(x * x, axis=-1, keepdims=True) + EPS)
            ext[start + b : start + b + n, :] = (x * scale * gain).astype(BF16)
    normed_ref[0] = ext[HALO:, :]
    for k in range(1, CONV):
        mask[k - 1] = jnp.broadcast_to(same_ref[0, :, k : k + 1], (length, 128))

    def tile(c):
        cols = pl.ds(pl.multiple_of(c * TILE, TILE), TILE)
        low = nn(ext[...], wraw_ref[:, cols]).astype(BF16)
        raw_ref[0, :, cols] = low
        rawbuf[...] = low.astype(F32)
        for half in range(0, TILE, 128):
            hc = pl.ds(pl.multiple_of(c * TILE + half, 128), 128)
            w = cw_ref[:, hc]
            bias = cb_ref[:, hc]
            for b in range(0, length, 64):
                z = bias + w[3:4] * rawbuf[HALO + b : HALO + b + 64, half : half + 128]
                for j in range(1, CONV):
                    moved = rawbuf[HALO + b - j : HALO + b - j + 64, half : half + 128]
                    z = z + w[3 - j : 4 - j] * (moved * mask[j - 1, b : b + 64, :])
                sig = 1.0 / (1.0 + jnp.exp(-z))
                act[b : b + 64, half : half + 128] = z * sig
                dsilu_ref[0, b : b + 64, hc] = (sig * (1.0 + z * (1.0 - sig))).astype(BF16)

    def value_tile(c, carry):
        tile(c)
        val_ref[0, pl.ds(pl.multiple_of(c * TILE, TILE), TILE), :] = act[...].T.astype(BF16)
        return carry

    lax.fori_loop(0, INNER // TILE, value_tile, 0)
    tile(INNER // TILE)
    wr_ref[0] = act[...].astype(BF16)

    draw = nt(dlow_ref[...], ext[HALO:, :]) + bias_ref[...]
    delta = softplus(draw)
    draw_ref[0] = draw
    delta_ref[0] = delta
    totals = nn_high(-jnp.exp(rate_ref[...]) * delta, triangle(length))
    seg = segrow_ref[0]
    keep = jnp.where(seg == seg[:, length - 1 :], 1.0, 0.0)
    weight[...] = jnp.exp(totals[:, length - 1 :] - totals) * keep * delta
    writers = wr_ref[0, :, :STATE]

    def state_tile(c, carry):
        for h in range(4):
            rows = pl.ds(pl.multiple_of(c * TILE + h * HEADDIM, HEADDIM), HEADDIM)
            act_t = val_ref[0, rows, :].astype(F32) * weight[pl.ds(c * 4 + h, 1), :]
            send_ref[0, rows, :] = nn(act_t.astype(BF16), writers).astype(BF16)
        return carry

    lax.fori_loop(0, INNER // TILE, state_tile, 0)


def enter(tokens, halo, gain, wraw, dlow, cw, cb, same, bias, rate, segrow):
    n, length, _ = tokens.shape
    one = lambda *shape: pl.BlockSpec((1,) + shape, lambda i: (i, 0, 0))
    whole = lambda a: pl.BlockSpec(a.shape, lambda i: (0,) * a.ndim)
    outs = [
        ((n, length, D), BF16),
        ((n, length + HALO, XBC), BF16),
        ((n, length, XBC), BF16),
        ((n, INNER, length), BF16),
        ((n, length, 2 * STATE), BF16),
        ((n, HP, length), F32),
        ((n, HP, length), F32),
        ((n, INNER, STATE), BF16),
    ]
    return pl.pallas_call(
        enter_kernel,
        grid=(n,),
        in_specs=[
            one(length, D), one(HALO, D), whole(gain), whole(wraw), whole(dlow), whole(cw),
            whole(cb), one(length, 8), whole(bias), whole(rate), one(1, length),
        ],
        out_specs=[one(*s[1:]) for s, _ in outs],
        out_shape=[jax.ShapeDtypeStruct(s, t) for s, t in outs],
        scratch_shapes=[
            pltpu.VMEM((length + HALO, D), BF16),
            pltpu.VMEM((length + HALO, TILE), F32),
            pltpu.VMEM((length, TILE), F32),
            pltpu.VMEM((CONV - 1, length, 128), F32),
            pltpu.VMEM((HP, length), F32),
        ],
        compiler_params=params(("arbitrary",)),
        name="enter",
    )(tokens, halo, gain, wraw, dlow, cw, cb, same, bias, rate, segrow)


def chunk_terms(delta, rate_ref, segrow, segcol, before, last):
    decay = -jnp.exp(rate_ref[...]) * delta
    totals = nn_high(decay, triangle(CH))
    end = totals[:, CH - 1 :]
    fade = jnp.exp(totals) * jnp.where(segrow == before, 1.0, 0.0)
    to_end = jnp.exp(end - totals) * jnp.where(segrow == last, 1.0, 0.0)
    passing = jnp.exp(end) * jnp.where(last == before, 1.0, 0.0)
    allowed = (segcol == segrow) & (
        lax.broadcasted_iota(jnp.int32, (CH, CH), 0)
        <= lax.broadcasted_iota(jnp.int32, (CH, CH), 1)
    )
    return decay, totals, fade, to_end, passing, jnp.where(allowed, 0.0, NEG)


def forward_kernel(
    marks_ref, val_ref, w_ref, r_ref, delta_ref, rate_ref, segrow_ref, segcol_ref, in_ref,
    y_ref, start_ref,
    state, off, fresh,
):
    n, k = pl.program_id(0), pl.program_id(1)

    @pl.when(k == 0)
    def _():
        state[...] = in_ref[0].astype(F32)

    writers, readers = w_ref[0], r_ref[0]
    delta = delta_ref[0]
    _, totals, fade, to_end, passing, barred = chunk_terms(
        delta, rate_ref, segrow_ref[0], segcol_ref[0], marks_ref[n, k, 0], marks_ref[n, k, 1]
    )
    columns = totals.T
    scores = nt(writers, readers)
    low_state = state[...].astype(BF16)
    start_ref[0, 0] = low_state
    off[...] = nt(low_state, readers)
    for h in range(HEADS):
        rows = slice(h * HEADDIM, (h + 1) * HEADDIM)
        mixing = jnp.exp(totals[h : h + 1, :] - columns[:, h : h + 1] + barred) * scores
        scaled = val_ref[0, rows, :].astype(F32) * delta[h : h + 1, :]
        fresh[rows, :] = (scaled * to_end[h : h + 1, :]).astype(BF16)
        inside = nn(scaled.astype(BF16), mixing.astype(BF16))
        y_ref[0, rows, :] = inside + off[rows, :] * fade[h : h + 1, :]
    off[...] = nn(fresh[...], writers)
    for h in range(HEADS):
        rows = slice(h * HEADDIM, (h + 1) * HEADDIM)
        state[rows, :] = passing[h : h + 1, :] * state[rows, :] + off[rows, :]


def forward_scan(marks, values, wr, delta, rate, segrow, segcol, incoming):
    n, _, length = values.shape
    chunks = length // CH
    return pl.pallas_call(
        forward_kernel,
        grid_spec=pltpu.PrefetchScalarGridSpec(
            num_scalar_prefetch=1,
            grid=(n, chunks),
            in_specs=[
                pl.BlockSpec((1, INNER, CH), lambda i, k, m: (i, 0, k)),
                pl.BlockSpec((1, CH, STATE), lambda i, k, m: (i, k, 0)),
                pl.BlockSpec((1, CH, STATE), lambda i, k, m: (i, k, 1)),
                pl.BlockSpec((1, HP, CH), lambda i, k, m: (i, 0, k)),
                pl.BlockSpec((HP, 1), lambda i, k, m: (0, 0)),
                pl.BlockSpec((1, 1, CH), lambda i, k, m: (i, 0, k)),
                pl.BlockSpec((1, CH, 1), lambda i, k, m: (i, k, 0)),
                pl.BlockSpec((1, INNER, STATE), lambda i, k, m: (i, 0, 0)),
            ],
            out_specs=[
                pl.BlockSpec((1, INNER, CH), lambda i, k, m: (i, 0, k)),
                pl.BlockSpec((1, 1, INNER, STATE), lambda i, k, m: (i, k, 0, 0)),
            ],
            scratch_shapes=[
                pltpu.VMEM((INNER, STATE), F32),
                pltpu.VMEM((INNER, CH), F32),
                pltpu.VMEM((INNER, CH), BF16),
            ],
        ),
        out_shape=[
            jax.ShapeDtypeStruct((n, INNER, length), F32),
            jax.ShapeDtypeStruct((n, chunks, INNER, STATE), BF16),
        ],
        compiler_params=params(("arbitrary", "arbitrary")),
        name="forward_scan",
    )(marks, values, wr, wr, delta, rate, segrow, segcol, incoming)


def backward_kernel(
    marks_ref, val_ref, w_ref, r_ref, delta_ref, draw_ref, rate_ref, skip_ref, segrow_ref,
    segcol_ref, gy_ref, first_ref, start_ref, in_ref, carry_ref,
    gval_ref, gwr_ref, gdraw_ref, gbias_ref, grate_ref,
    grad, link, off, fresh, faded, gdelta, paid,
):
    n, step = pl.program_id(0), pl.program_id(1)
    k = pl.num_programs(1) - 1 - step

    @pl.when(step == 0)
    def _():
        grad[...] = in_ref[0].astype(F32)
        link[...] = carry_ref[0]

    @pl.when((n == 0) & (step == 0))
    def _():
        gbias_ref[...] = jnp.zeros_like(gbias_ref)
        grate_ref[...] = jnp.zeros_like(grate_ref)

    writers, readers = w_ref[0], r_ref[0]
    delta = delta_ref[0]
    segrow, segcol = segrow_ref[0], segcol_ref[0]
    decay, totals, fade, to_end, passing, barred = chunk_terms(
        delta, rate_ref, segrow, segcol, marks_ref[n, k, 0], marks_ref[n, k, 1]
    )
    columns = totals.T
    scores = nt(writers, readers)
    low_grad = grad[...].astype(BF16)
    off[...] = nt(low_grad, writers)
    gscores = jnp.zeros((CH, CH), F32)
    gdelta[...] = jnp.zeros_like(gdelta)
    paid[...] = jnp.zeros_like(paid)
    for h in range(HEADS):
        rows = slice(h * HEADDIM, (h + 1) * HEADDIM)
        spread = jnp.exp(totals[h : h + 1, :] - columns[:, h : h + 1] + barred)
        values = val_ref[0, rows, :].astype(F32)
        gy = gy_ref[0, rows, :]
        gy32 = gy.astype(F32)
        scaled = values * delta[h : h + 1, :]
        fresh[rows, :] = (scaled * to_end[h : h + 1, :]).astype(BF16)
        faded[rows, :] = (gy32 * fade[h : h + 1, :]).astype(BF16)
        gscaled = nt(gy, (spread * scores).astype(BF16)) + off[rows, :] * to_end[h : h + 1, :]
        low = scaled.astype(BF16)
        gscores = gscores + tn(low, gy) * spread
        paid[h : h + 1, :] = jnp.sum(low.astype(F32) * gscaled, axis=0, keepdims=True)
        gdelta[h : h + 1, :] = jnp.sum(values * gscaled, axis=0, keepdims=True)
        gval_ref[0, rows, :] = (
            gscaled * delta[h : h + 1, :] + gy32 * skip_ref[h : h + 1, :]
        ).astype(BF16)
    low_scores = gscores.astype(BF16)
    gwr_ref[0, :, :STATE] = nn(low_scores, readers) + tn(fresh[...], low_grad)
    gwr_ref[0, :, STATE:] = tn(low_scores, writers) + tn(faded[...], start_ref[0, 0])
    off[...] = nn(faded[...], readers)
    for h in range(HEADS):
        rows = slice(h * HEADDIM, (h + 1) * HEADDIM)
        grad[rows, :] = passing[h : h + 1, :] * grad[rows, :] + off[rows, :]
    difference = first_ref[0] - paid[...]
    reach = jnp.where(
        (segcol == segrow)
        & (
            lax.broadcasted_iota(jnp.int32, (CH, CH), 0)
            >= lax.broadcasted_iota(jnp.int32, (CH, CH), 1)
        ),
        1.0,
        0.0,
    )
    following = jnp.where(segrow == marks_ref[n, k, 2], 1.0, 0.0)
    gdecay = nn_high(difference, reach) + following * link[...]
    link[...] = gdecay[:, :1]
    gtotal = gdelta[...] - jnp.exp(rate_ref[...]) * gdecay
    gdraw = gtotal / (1.0 + jnp.exp(-draw_ref[0]))
    gdraw_ref[0] = gdraw
    gbias_ref[...] += jnp.sum(gdraw, axis=1, keepdims=True)
    grate_ref[...] += jnp.sum(gdecay * decay, axis=1, keepdims=True)


def backward_scan(
    marks, values, wr, delta, draw, rate, skip, segrow, segcol, gy, first, starts, incoming, carry
):
    n, _, length = values.shape
    chunks = length // CH
    back = lambda k: chunks - 1 - k
    lanes = lambda rows: pl.BlockSpec((1, rows, CH), lambda i, k, m: (i, 0, back(k)))
    column = pl.BlockSpec((HP, 1), lambda i, k, m: (0, 0))
    return pl.pallas_call(
        backward_kernel,
        grid_spec=pltpu.PrefetchScalarGridSpec(
            num_scalar_prefetch=1,
            grid=(n, chunks),
            in_specs=[
                lanes(INNER),
                pl.BlockSpec((1, CH, STATE), lambda i, k, m: (i, back(k), 0)),
                pl.BlockSpec((1, CH, STATE), lambda i, k, m: (i, back(k), 1)),
                lanes(HP),
                lanes(HP),
                column,
                column,
                lanes(1),
                pl.BlockSpec((1, CH, 1), lambda i, k, m: (i, back(k), 0)),
                lanes(INNER),
                lanes(HP),
                pl.BlockSpec((1, 1, INNER, STATE), lambda i, k, m: (i, back(k), 0, 0)),
                pl.BlockSpec((1, INNER, STATE), lambda i, k, m: (i, 0, 0)),
                pl.BlockSpec((1, HP, 1), lambda i, k, m: (i, 0, 0)),
            ],
            out_specs=[
                lanes(INNER),
                pl.BlockSpec((1, CH, 2 * STATE), lambda i, k, m: (i, back(k), 0)),
                lanes(HP),
                column,
                column,
            ],
            scratch_shapes=[
                pltpu.VMEM((INNER, STATE), F32),
                pltpu.VMEM((HP, 1), F32),
                pltpu.VMEM((INNER, CH), F32),
                pltpu.VMEM((INNER, CH), BF16),
                pltpu.VMEM((INNER, CH), BF16),
                pltpu.VMEM((HP, CH), F32),
                pltpu.VMEM((HP, CH), F32),
            ],
        ),
        out_shape=[
            jax.ShapeDtypeStruct((n, INNER, length), BF16),
            jax.ShapeDtypeStruct((n, length, 2 * STATE), F32),
            jax.ShapeDtypeStruct((n, HP, length), F32),
            jax.ShapeDtypeStruct((HP, 1), F32),
            jax.ShapeDtypeStruct((HP, 1), F32),
        ],
        compiler_params=params(("arbitrary", "arbitrary")),
        name="backward_scan",
    )(
        marks, values, wr, wr, delta, draw, rate, skip, segrow, segcol, gy, first, starts,
        incoming, carry,
    )


def leave_kernel(
    marks_ref, normed_ref, wgate_ref, wout_ref, cot_ref, tok_ref, y_ref, val_ref, r_ref,
    gain_ref, skip_ref, delta_ref, rate_ref, segrow_ref,
    out_ref, gy_ref, ggate_ref, first_ref, gstate_ref, gout_ref, ggain_ref, gskip_ref,
    gate, gated, upward, lifted, flat, fade, total, products, skips,
):
    n = pl.program_id(0)
    length = normed_ref.shape[1]
    tiles = INNER // TILE
    lanes = range(0, length, 128)

    @pl.when(n == 0)
    def _():
        total[...] = jnp.zeros_like(total)
        ggain_ref[...] = jnp.zeros_like(ggain_ref)
        skips[...] = jnp.zeros_like(skips)

    totals = nn_high(-jnp.exp(rate_ref[...]) * delta_ref[0], triangle(length))
    fade[...] = jnp.exp(totals) * jnp.where(segrow_ref[0] == marks_ref[n, 0, 0], 1.0, 0.0)

    def fold(v):
        return jnp.sum(v.reshape(HEADDIM // 8, 8, 128), axis=0)

    def span(c):
        return pl.ds(pl.multiple_of(c * TILE, TILE), TILE)

    def head_rows(c, h):
        return pl.ds(pl.multiple_of(c * TILE + h * HEADDIM, HEADDIM), HEADDIM)

    def gate_tile(c, squares):
        gate[span(c), :] = nn(normed_ref[0], wgate_ref[:, span(c)]).T.astype(BF16)
        parts = list(squares)
        for h in range(4):
            rows = head_rows(c, h)
            skip = skip_ref[pl.ds(c * 4 + h, 1), :]
            for i, b in enumerate(lanes):
                g = gate[rows, b : b + 128].astype(F32)
                values = val_ref[0, rows, b : b + 128].astype(F32)
                v = (y_ref[0, rows, b : b + 128] + skip * values) * (g / (1.0 + jnp.exp(-g)))
                gated[rows, b : b + 128] = v
                parts[i] = parts[i] + fold(v * v)
        return tuple(parts)

    zero = tuple(jnp.zeros((8, 128), F32) for _ in lanes)
    down = lambda s: jnp.sum(s, axis=0, keepdims=True)
    squares = lax.fori_loop(0, tiles, gate_tile, zero)
    scale = [lax.rsqrt(down(s) * (1.0 / INNER) + EPS) for s in squares]

    def norm_tile(c, dots):
        upward[span(c), :] = nt(wout_ref[span(c), :], cot_ref[0])
        parts = list(dots)
        for h in range(4):
            rows = head_rows(c, h)
            gain = gain_ref[rows, :]
            sums = jnp.zeros((HEADDIM, 128), F32)
            for i, b in enumerate(lanes):
                v = gated[rows, b : b + 128]
                normal = v * scale[i]
                lifted[rows, b : b + 128] = (normal * gain).astype(BF16)
                u = upward[rows, b : b + 128]
                sums = sums + u * normal
                u = u * gain
                upward[rows, b : b + 128] = u
                parts[i] = parts[i] + fold(u * v)
            ggain_ref[rows, :] += jnp.sum(sums, axis=1, keepdims=True)
        low = lifted[span(c), :]
        flat[:, span(c)] = low.T
        total[span(c), :] += nn(low, cot_ref[0])
        return tuple(parts)

    dots = lax.fori_loop(0, tiles, norm_tile, zero)
    pull = [s * s * s * down(d) * (1.0 / INNER) for s, d in zip(scale, dots)]
    def back_tile(c, carry):
        for h in range(4):
            rows = head_rows(c, h)
            head = pl.ds(c * 4 + h, 1)
            eight = pl.ds(pl.multiple_of((c * 4 + h) * 8, 8), 8)
            skip = skip_ref[head, :]
            fading = fade[head, :]
            sums = jnp.zeros((8, 128), F32)
            for i, b in enumerate(lanes):
                gv = scale[i] * upward[rows, b : b + 128] - pull[i] * gated[rows, b : b + 128]
                g = gate[rows, b : b + 128].astype(F32)
                sig = 1.0 / (1.0 + jnp.exp(-g))
                silu = g * sig
                values = val_ref[0, rows, b : b + 128].astype(F32)
                y = y_ref[0, rows, b : b + 128]
                low = (gv * silu).astype(BF16)
                gm = low.astype(F32)
                ggate_ref[0, rows, b : b + 128] = (
                    gv * (y + skip * values) * (sig + silu * (1.0 - sig))
                ).astype(BF16)
                gy_ref[0, rows, b : b + 128] = low
                products[eight, b : b + 128] = fold(gm * y)
                sums = sums + fold(gm * values)
                lifted[rows, b : b + 128] = (gm * fading[:, b : b + 128]).astype(BF16)
            skips[eight, :] += sums
        gstate_ref[0, span(c), :] = nn(lifted[span(c), :], r_ref[0]).astype(BF16)
        return carry

    lax.fori_loop(0, tiles, back_tile, 0)
    first_ref[0, 0:HEADS, :] = jnp.sum(products[...].reshape(HEADS, 8, length), axis=1)
    first_ref[0, HEADS:, :] = jnp.zeros((HP - HEADS, length), F32)
    for b in range(0, D, TILE):
        branch = nn(flat[...], wout_ref[:, b : b + TILE])
        out_ref[0, :, b : b + TILE] = (tok_ref[0, :, b : b + TILE].astype(F32) + branch).astype(BF16)

    @pl.when(n == pl.num_programs(0) - 1)
    def _():
        gout_ref[...] = total[...].astype(BF16)
        gskip_ref[0:HEADS, :] = jnp.sum(skips[...].reshape(HEADS, 8, 128), axis=1)
        gskip_ref[HEADS:, :] = jnp.zeros((HP - HEADS, 128), F32)


def leave(
    marks, normed, wgate, wout, cot, tokens, y, values, wr, gain, skip, delta, rate, segrow
):
    n, length, _ = normed.shape
    one = lambda *shape: pl.BlockSpec((1,) + shape, lambda i, m: (i, 0, 0))
    whole = lambda a: pl.BlockSpec(a.shape, lambda i, m: (0,) * a.ndim)
    flat = lambda *shape: pl.BlockSpec(shape, lambda i, m: (0, 0))
    return pl.pallas_call(
        leave_kernel,
        grid_spec=pltpu.PrefetchScalarGridSpec(
            num_scalar_prefetch=1,
            grid=(n,),
            in_specs=[
                one(length, D), whole(wgate), whole(wout), one(length, D), one(length, D),
                one(INNER, length), one(INNER, length),
                pl.BlockSpec((1, length, STATE), lambda i, m: (i, 0, 1)),
                whole(gain), whole(skip), one(HP, length), whole(rate), one(1, length),
            ],
            out_specs=[
                one(length, D), one(INNER, length), one(INNER, length), one(HP, length),
                one(INNER, STATE), flat(INNER, D), flat(INNER, 1), flat(HP, 128),
            ],
            scratch_shapes=[
                pltpu.VMEM((INNER, length), BF16),
                pltpu.VMEM((INNER, length), F32),
                pltpu.VMEM((INNER, length), F32),
                pltpu.VMEM((INNER, length), BF16),
                pltpu.VMEM((length, INNER), BF16),
                pltpu.VMEM((HP, length), F32),
                pltpu.VMEM((INNER, D), F32),
                pltpu.VMEM((HEADS * 8, length), F32),
                pltpu.VMEM((HEADS * 8, 128), F32),
            ],
        ),
        out_shape=[
            jax.ShapeDtypeStruct((n, length, D), BF16),
            jax.ShapeDtypeStruct((n, INNER, length), BF16),
            jax.ShapeDtypeStruct((n, INNER, length), BF16),
            jax.ShapeDtypeStruct((n, HP, length), F32),
            jax.ShapeDtypeStruct((n, INNER, STATE), BF16),
            jax.ShapeDtypeStruct((INNER, D), BF16),
            jax.ShapeDtypeStruct((INNER, 1), F32),
            jax.ShapeDtypeStruct((HP, 128), F32),
        ],
        compiler_params=params(("arbitrary",)),
        name="leave",
    )(marks, normed, wgate, wout, cot, tokens, y, values, wr, gain, skip, delta, rate, segrow)


def conv_back_kernel(
    gval_ref, gwr_ref, dsilu_ref, raw_ref, near_ref, cw_ref,
    graw_ref, tail_ref, ghalo_ref, gconv_ref,
    pre, rawbuf, mask,
):
    c, n = pl.program_id(0), pl.program_id(1)
    length = dsilu_ref.shape[1]

    @pl.when(n == 0)
    def _():
        gconv_ref[...] = jnp.zeros_like(gconv_ref)

    for j in range(1, CONV):
        mask[j - 1] = jnp.broadcast_to(near_ref[0, :, j : j + 1], (length + 8, 128))
    pre[0:8, :] = jnp.zeros((8, TILE), F32)
    pre[length + 8 :, :] = jnp.zeros((8, TILE), F32)

    @pl.when(c < INNER // TILE)
    def _():
        pre[8 : length + 8, :] = gval_ref[0].astype(F32).T

    @pl.when(c == INNER // TILE)
    def _():
        pre[8 : length + 8, :] = gwr_ref[0]

    rawbuf[...] = raw_ref[0].astype(F32)
    for half in range(0, TILE, 128):
        cols = slice(half, half + 128)
        w = cw_ref[:, cols]
        for b in range(0, length, 64):
            pre[8 + b : 72 + b, cols] = pre[8 + b : 72 + b, cols] * dsilu_ref[0, b : b + 64, cols].astype(F32)
        sums = [jnp.zeros((8, 128), F32) for _ in range(CONV + 1)]
        for b, rows in [(0, 8)] + [(8 + 64 * i, 64) for i in range(length // 64)]:
            fold = lambda v: jnp.sum(v.reshape(rows // 8, 8, 128), axis=0)
            raw = rawbuf[HALO - 8 + b : HALO - 8 + b + rows, cols]
            here = pre[b : b + rows, cols]
            grad = w[3:4] * here
            sums[3] = sums[3] + fold(raw * here)
            sums[4] = sums[4] + fold(here)
            for j in range(1, CONV):
                term = pre[b + j : b + j + rows, cols] * mask[j - 1, b : b + rows, :]
                grad = grad + w[3 - j : 4 - j] * term
                sums[3 - j] = sums[3 - j] + fold(raw * term)
            if b == 0:
                ghalo_ref[0, :, cols] = grad
            else:
                graw_ref[0, b - 8 : b - 8 + rows, cols] = grad.astype(BF16)
        tail_ref[0, :, cols] = grad[48:]
        gconv_ref[0 : CONV + 1, cols] += jnp.concatenate(
            [jnp.sum(s, axis=0, keepdims=True) for s in sums], axis=0
        )


def conv_back(gval, gwr, dsilu, raw, near, cw):
    n, length, _ = dsilu.shape
    tiles = XBC // TILE
    rows = lambda r: pl.BlockSpec((1, r, TILE), lambda c, i: (i, 0, c))
    return pl.pallas_call(
        conv_back_kernel,
        grid=(tiles, n),
        in_specs=[
            pl.BlockSpec((1, TILE, length), lambda c, i: (i, jnp.minimum(c, INNER // TILE - 1), 0)),
            pl.BlockSpec((1, length, TILE), lambda c, i: (i, 0, 0)),
            rows(length),
            rows(length + HALO),
            pl.BlockSpec((1, length + 8, 8), lambda c, i: (i, 0, 0)),
            pl.BlockSpec((8, TILE), lambda c, i: (0, c)),
        ],
        out_specs=[
            rows(length), rows(16), rows(8), pl.BlockSpec((8, TILE), lambda c, i: (0, c)),
        ],
        out_shape=[
            jax.ShapeDtypeStruct((n, length, XBC), BF16),
            jax.ShapeDtypeStruct((n, 16, XBC), F32),
            jax.ShapeDtypeStruct((n, 8, XBC), F32),
            jax.ShapeDtypeStruct((8, XBC), F32),
        ],
        scratch_shapes=[
            pltpu.VMEM((length + 16, TILE), F32),
            pltpu.VMEM((length + HALO, TILE), F32),
            pltpu.VMEM((CONV - 1, length + 8, 128), F32),
        ],
        compiler_params=params(("arbitrary", "arbitrary")),
        name="conv_back",
    )(gval, gwr, dsilu, raw, near, cw)


MESH = pl.DeviceIdType.MESH


def sum_kernel(
    width, group, replicas, x_ref, o_ref, own, from_group, from_reps,
    send_a, recv_a, send_b, recv_b, send_c, recv_c,
):
    r, f, s = lax.axis_index("rep"), lax.axis_index("fsdp"), lax.axis_index("seq")
    me = f * 2 + s
    peers = []
    for j in range(1, group):
        p = lax.rem(me + j, group)
        peers.append((p, (r, lax.div(p, 2), lax.rem(p, 2))))
    others = [(lax.rem(r + j, replicas), f, s) for j in range(1, replicas)]
    barrier = pltpu.get_barrier_semaphore()
    for device in [d for _, d in peers] + others:
        pl.semaphore_signal(barrier, inc=1, device_id=device, device_id_type=MESH)
    pl.semaphore_wait(barrier, group + replicas - 2)

    sent = []
    for j, (p, device) in enumerate(peers):
        copy = pltpu.make_async_remote_copy(
            x_ref.at[pl.ds(p * width, width)], from_group.at[j], send_a.at[j], recv_a.at[j],
            device_id=device, device_id_type=MESH,
        )
        copy.start()
        sent.append(copy)
    total = x_ref[pl.ds(me * width, width)]
    for j in range(group - 1):
        sent[j].wait_recv()
        total = total + from_group[j]
    own[...] = total
    from_reps[pl.ds(r, 1)] = total[None]
    for j, device in enumerate(others):
        copy = pltpu.make_async_remote_copy(
            own, from_reps.at[r], send_b.at[j], recv_b.at[j], device_id=device, device_id_type=MESH
        )
        copy.start()
        sent.append(copy)
    for j in range(replicas - 1):
        sent[group - 1 + j].wait_recv()
    total = from_reps[0]
    for j in range(1, replicas):
        total = total + from_reps[j]
    mine = pl.ds(me * width, width)
    o_ref[mine] = total
    shared = []
    for j, (p, device) in enumerate(peers):
        copy = pltpu.make_async_remote_copy(
            o_ref.at[mine], o_ref.at[mine], send_c.at[j], recv_c.at[j],
            device_id=device, device_id_type=MESH,
        )
        copy.start()
        shared.append(copy)
    for copy in sent:
        copy.wait_send()
    for copy in shared:
        copy.wait()


def sum_everywhere(tiles, identity):
    group = lax.axis_size("fsdp") * lax.axis_size("seq")
    replicas = lax.axis_size("rep")
    width = tiles.shape[0] // group
    block = (width, 8, 128)
    dma = pltpu.SemaphoreType.DMA
    return pl.pallas_call(
        partial(sum_kernel, width, group, replicas),
        out_shape=jax.ShapeDtypeStruct(tiles.shape, F32),
        in_specs=[pl.BlockSpec(memory_space=pltpu.VMEM)],
        out_specs=pl.BlockSpec(memory_space=pltpu.VMEM),
        scratch_shapes=[
            pltpu.VMEM(block, F32),
            pltpu.VMEM((group - 1,) + block, F32),
            pltpu.VMEM((replicas,) + block, F32),
            dma((group - 1,)), dma((group - 1,)),
            dma((replicas - 1,)), dma((replicas - 1,)),
            dma((group - 1,)), dma((group - 1,)),
        ],
        compiler_params=pltpu.CompilerParams(collective_id=identity, has_side_effects=True),
        name="sum_everywhere",
    )(tiles)


def split_three(v):
    high = v.astype(BF16)
    rest = v - high.astype(F32)
    middle = rest.astype(BF16)
    return [high, middle, (rest - middle.astype(F32)).astype(BF16)]


def join_three(v):
    return v[0:8] + v[8:16] + v[16:24]


def tiles_of(extent):
    return -(-extent // 128)


def pieces_of(rows):
    return [(i, i * 128, min(128, rows - i * 128)) for i in range(tiles_of(rows))]


def left_kernel(me_ref, sin_ref, sout_ref, gate_ref, raw_ref, out_ref, err_ref, x_ref):
    group, rows_in, rows_out = gate_ref.shape[0], gate_ref.shape[1], out_ref.shape[1]
    ahead = tiles_of(rows_in)
    width = ahead + tiles_of(rows_out)
    x_ref[...] = jnp.zeros_like(x_ref)
    for p in range(group):
        left = join_three(nt(sin_ref[:, :INNER], gate_ref[p]) + nt(sin_ref[:, INNER:], raw_ref[p]))
        for i, at, n in pieces_of(rows_in):
            x_ref[p * width + i, :, :n] = left[:, at : at + n]
        left = join_three(nt(sout_ref[...], out_ref[p]))
        for i, at, n in pieces_of(rows_out):
            x_ref[p * width + ahead + i, :, :n] = left[:, at : at + n]
    mine = pl.ds(me_ref[0] * width, width)
    x_ref[mine] = x_ref[mine] + err_ref[...]


def inverse_factor(gram):
    rows = lax.broadcasted_iota(jnp.int32, (8, 8), 0)
    cols = lax.broadcasted_iota(jnp.int32, (8, 8), 1)
    left, right = gram, jnp.where(rows == cols, 1.0, 0.0)
    for j in range(7):
        factor = jnp.where(rows[:, :1] > j, left[:, j : j + 1] / left[j : j + 1, j : j + 1], 0.0)
        left, right = left - factor * left[j : j + 1, :], right - factor * right[j : j + 1, :]
    pivots = jnp.sum(jnp.where(rows == cols, left, 0.0), axis=1, keepdims=True)
    return right * lax.rsqrt(pivots)


def nt_high(a, b):
    return lax.dot_general(
        a, b, (((1,), (1,)), ((), ())), precision=HIGH, preferred_element_type=F32
    )


def tn_high(a, b):
    return lax.dot_general(
        a, b, (((0,), (0,)), ((), ())), precision=HIGH, preferred_element_type=F32
    )


def right_kernel(
    replicas, me_ref, left_ref, gate_ref, raw_ref, out_ref, ein_ref, eout_ref, small_ref,
    x_ref, own_ref,
    hat,
):
    group, rows_in, rows_out = gate_ref.shape[0], gate_ref.shape[1], out_ref.shape[1]
    ahead = tiles_of(rows_in)
    width = ahead + tiles_of(rows_out)
    for first, last in ((0, ahead), (ahead, width)):
        gram = jnp.zeros((8, 8), F32)
        for p in range(group):
            for i in range(first, last):
                tile = left_ref[p * width + i] * (1.0 / replicas)
                gram = gram + nt_high(tile, tile)
        inverse = inverse_factor(gram)
        for p in range(group):
            for i in range(first, last):
                hat[p * width + i] = nn_high(inverse, left_ref[p * width + i] * (1.0 / replicas))
    mine = pl.ds(me_ref[0] * width, width)
    own = hat[mine]
    own_ref[...] = own

    def product(matrices, rows, skipped, error, columns, at):
        spread = [
            jnp.concatenate(split_three(joined(hat, p * width + skipped, rows)), axis=0)
            for p in range(group)
        ]
        mixed = joined(own, skipped, rows)
        for ref, width_here in matrices:
            for b in range(0, width_here, TILE):
                total = jnp.zeros((24, TILE), F32)
                for p in range(group):
                    total = total + nn(spread[p], ref[p, :, b : b + TILE])
                right = join_three(total) + nn_high(mixed, error[:, columns + b : columns + b + TILE])
                for half in range(0, TILE, 128):
                    x_ref[at + (columns + b + half) // 128] = right[:, half : half + 128]
            columns += width_here

    def joined(tiles, start, rows):
        return jnp.concatenate([tiles[start + i][:, :n] for i, _, n in pieces_of(rows)], axis=1)

    product(((gate_ref, INNER), (raw_ref, XBC)), rows_in, 0, ein_ref, 0, 0)
    product(((out_ref, D),), rows_out, ahead, eout_ref, 0, PROJ // 128)
    after = (PROJ + D) // 128
    x_ref[after:] = jnp.zeros((x_ref.shape[0] - after, 8, 128), F32)
    x_ref[after : after + small_ref.shape[0]] = small_ref[...]


def update_kernel(
    rates, replicas, x_ref, own_ref, win_ref, wout_ref, min_ref, mout_ref,
    nwin_ref, nwout_ref, nmin_ref, nmout_ref,
):
    ahead = tiles_of(win_ref.shape[0])
    for w, m, nw, nm, first, columns, at, rate in (
        (win_ref, min_ref, nwin_ref, nmin_ref, 0, PROJ, 0, rates[0]),
        (wout_ref, mout_ref, nwout_ref, nmout_ref, ahead, D, PROJ // 128, rates[1]),
    ):
        for i, start, n in pieces_of(w.shape[0]):
            rows = slice(start, start + n)
            left = own_ref[first + i][:, :n]
            for b in range(0, columns, 128):
                approx = tn_high(left, x_ref[at + b // 128] * (1.0 / replicas))
                momentum = MOMENTUM * m[rows, b : b + 128] + approx
                nm[rows, b : b + 128] = momentum
                nw[rows, b : b + 128] = w[rows, b : b + 128] - rate * momentum


def residual_kernel(
    replicas, x_ref, own_ref, gate_ref, raw_ref, out_ref, ein_ref, eout_ref, nein_ref, neout_ref
):
    ahead = tiles_of(ein_ref.shape[0])
    for grad, error, new, first, columns, at, offset in (
        (gate_ref, ein_ref, nein_ref, 0, INNER, 0, 0),
        (raw_ref, ein_ref, nein_ref, 0, XBC, INNER // 128, INNER),
        (out_ref, eout_ref, neout_ref, ahead, D, PROJ // 128, 0),
    ):
        for i, start, n in pieces_of(error.shape[0]):
            rows = slice(start, start + n)
            left = own_ref[first + i][:, :n]
            for b in range(0, columns, 128):
                approx = tn_high(left, x_ref[at + b // 128] * (1.0 / replicas))
                here = slice(offset + b, offset + b + 128)
                new[rows, here] = (grad[rows, b : b + 128].astype(F32) + error[rows, here]) - approx


def local_call(kernel, outs, *arrays, scalars=0, scratch=(), name):
    spec = pl.BlockSpec(memory_space=pltpu.VMEM)
    return pl.pallas_call(
        kernel,
        out_shape=outs,
        in_specs=[pl.BlockSpec(memory_space=pltpu.SMEM)] * scalars + [spec] * (len(arrays) - scalars),
        out_specs=jax.tree.map(lambda _: spec, outs),
        scratch_shapes=list(scratch),
        compiler_params=pltpu.CompilerParams(vmem_limit_bytes=VMEM_LIMIT),
        name=name,
    )(*arrays)


def split_small(small_values):
    pieces = []
    offset = 0
    for amount in (D, D * HEADS, CONV * XBC, XBC, INNER, HEADS, HEADS, HEADS):
        pieces.append(small_values[offset : offset + amount])
        offset = offset + amount
    return (
        pieces[0],
        pieces[1].reshape(D, HEADS),
        pieces[2].reshape(CONV, XBC),
        pieces[3],
        pieces[4],
        pieces[5],
        pieces[6],
        pieces[7],
    )


def step_rates(tokens_replica):
    grad_scale = 0.3 * math.sqrt(tokens_replica)
    return (
        0.5 / (math.sqrt(D) * grad_scale),
        0.5 / (math.sqrt(INNER) * grad_scale),
        0.1 / grad_scale,
    )


def to_later(block):
    return lax.ppermute(block, "seq", [(i, i + 1) for i in range(lax.axis_size("seq") - 1)])


def to_earlier(block):
    return lax.ppermute(block, "seq", [(i + 1, i) for i in range(lax.axis_size("seq") - 1)])


def head_column(values):
    return jnp.pad(values, (0, HP - HEADS)).reshape(HP, 1)


def gather_rows(shard):
    return lax.all_gather(shard, ("fsdp", "seq"), axis=0, tiled=True)


def scatter_rows(total):
    return lax.psum_scatter(total, ("fsdp", "seq"), scatter_dimension=0, tiled=True)


def body(
    tokens,
    cotangent,
    segments,
    input_weight,
    output_weight,
    small_values,
    input_momentum,
    output_momentum,
    small_momentum,
    input_error,
    output_error,
    input_start,
    output_start,
):
    shape = tokens.shape
    pieces = shape[0] * shape[1]
    length = shape[2]
    chunks = length // CH
    replicas = lax.axis_size("rep")
    place = lax.axis_index("seq")
    whole_length = segments.shape[2]
    tokens_replica = pieces * length * lax.axis_size("fsdp") * lax.axis_size("seq")
    rate_in, rate_out, rate_small = step_rates(tokens_replica)
    norm_gain, delta_weight, conv_weight, conv_bias, gate_gain, dt_bias, log_rate, skip_gain = (
        split_small(small_values)
    )
    raw_low = input_weight[:, INNER:].astype(BF16)
    gate_low = input_weight[:, :INNER].astype(BF16)
    raw_full = gather_rows(raw_low)
    gate_full = gather_rows(gate_low)
    output_full = gather_rows(output_weight.astype(BF16))

    tokens = tokens.reshape(pieces, length, D)
    cotangent = cotangent.reshape(pieces, length, D)
    documents = segments.reshape(pieces, whole_length)
    padded = jnp.pad(documents, ((0, 0), (HALO, 1)), constant_values=-1)
    wider = lax.dynamic_slice_in_dim(padded, place * length, HALO + length + 1, 1)
    own = wider[:, HALO : HALO + length]
    ahead = jnp.pad(wider[:, HALO - 8 : HALO + length], ((0, 0), (0, 8)), constant_values=-3)
    same = jnp.stack(
        [
            jnp.where(wider[:, HALO - j : HALO - j + length] == own, 1.0, 0.0)
            for j in range(CONV)
        ]
        + [jnp.zeros(own.shape, F32)] * (8 - CONV),
        axis=2,
    )
    near = jnp.stack(
        [
            jnp.where(ahead[:, j : j + length + 8] == ahead[:, : length + 8], 1.0, 0.0)
            for j in range(CONV)
        ]
        + [jnp.zeros((pieces, length + 8), F32)] * (8 - CONV),
        axis=2,
    )
    edges = wider[:, HALO - 1 :]
    marks = jnp.stack(
        [edges[:, :-2:CH], edges[:, CH::CH][:, :chunks], edges[:, CH + 1 :: CH]], axis=2
    )
    segrow = own[:, None, :]
    segcol = own[:, :, None]
    delta_low = delta_weight.astype(BF16)
    delta_rows = jnp.pad(delta_low.T, ((0, HP - HEADS), (0, 0)))
    taps = jnp.pad(conv_weight, ((0, 8 - CONV), (0, 0)))
    bias, rate, skip = head_column(dt_bias), head_column(log_rate), head_column(skip_gain)
    halo = to_later(tokens[:, length - HALO :, :])

    def error_tiles(error, start):
        left = nt_high(start.T, error[0])
        amount = tiles_of(left.shape[1])
        left = jnp.pad(left, ((0, 0), (0, amount * 128 - left.shape[1])))
        return left.reshape(8, amount, 128).transpose(1, 0, 2)

    error_left = jnp.concatenate(
        [error_tiles(input_error, input_start), error_tiles(output_error, output_start)], axis=0
    )
    start_in = jnp.concatenate(split_three(input_start.T), axis=0)
    start_out = jnp.concatenate(split_three(output_start.T), axis=0)

    normed, raw, dsilu, values, wr, draw, delta, send = enter(
        tokens, halo, norm_gain[None], raw_full, delta_rows, taps, conv_bias[None], same, bias,
        rate, segrow,
    )
    incoming = to_later(send)
    y, starts = forward_scan(marks, values, wr, delta, rate, segrow, segcol, incoming)
    output, gy, ggate, first, gstate, grad_output, ggain, gskip = leave(
        marks, normed, gate_full, output_full, cotangent, tokens, y, values, wr,
        gate_gain[:, None], skip, delta, rate, segrow,
    )
    output_total = scatter_rows(grad_output)
    outgoing = to_earlier(gstate)
    grad_gate = jnp.einsum("nld,nkl->dk", normed, ggate, preferred_element_type=F32).astype(BF16)
    gate_total = scatter_rows(grad_gate)
    carry = jnp.sum(
        (outgoing.astype(F32) * send.astype(F32)).reshape(pieces, HEADS, HEADDIM * STATE), axis=2
    )
    carry = jnp.pad(carry, ((0, 0), (0, HP - HEADS)))[:, :, None]
    gval, gwr, gdraw, gbias, grate = backward_scan(
        marks, values, wr, delta, draw, rate, skip, segrow, segcol, gy, first, starts, outgoing,
        carry,
    )
    graw, tail, ghalo, gconv = conv_back(gval, gwr, dsilu, raw, near, taps)
    returned = to_earlier(ghalo)
    tail = tail + jnp.pad(returned, ((0, 0), (8, 0), (0, 0)))
    graw = lax.dynamic_update_slice_in_dim(graw, tail.astype(BF16), length - 16, 1)
    grad_raw = jnp.einsum("nld,nlk->dk", normed, graw, preferred_element_type=F32).astype(BF16)
    raw_total = scatter_rows(grad_raw)
    gdelta = gdraw[:, :HEADS].astype(BF16)
    delta_weight_grad = jnp.einsum("nld,nhl->dh", normed, gdelta, preferred_element_type=F32)
    normed_grad = (
        jnp.einsum("nkl,dk->nld", ggate, gate_full, preferred_element_type=F32)
        + jnp.einsum("nlk,dk->nld", graw, raw_full, preferred_element_type=F32)
        + jnp.einsum("nhl,dh->nld", gdelta, delta_low, preferred_element_type=F32)
    )
    rows_in = tokens.astype(F32)
    scale = lax.rsqrt(jnp.mean(rows_in * rows_in, axis=-1, keepdims=True) + EPS)
    lifted = normed_grad * norm_gain
    norm_gain_grad = jnp.sum(normed_grad * rows_in * scale, axis=(0, 1))
    rows_grad = scale * lifted - rows_in * (
        scale * scale * scale * jnp.mean(lifted * rows_in, axis=-1, keepdims=True)
    )
    input_grad = (cotangent.astype(F32) + rows_grad).astype(BF16)
    small_total = jnp.concatenate(
        [
            norm_gain_grad,
            delta_weight_grad.reshape(-1),
            gconv[:CONV].reshape(-1),
            gconv[CONV],
            ggain[:, 0],
            gbias[:HEADS, 0],
            grate[:HEADS, 0],
            jnp.sum(gskip[:HEADS], axis=1),
        ]
    )
    group = lax.axis_size("fsdp") * lax.axis_size("seq")
    me = (lax.axis_index("fsdp") * lax.axis_size("seq") + place).astype(jnp.int32).reshape(1)
    tall = lambda tiles: jax.ShapeDtypeStruct((tiles, 8, 128), F32)
    like = lambda a: jax.ShapeDtypeStruct(a.shape, a.dtype)
    by_owner = lambda a: a.reshape(group, a.shape[0] // group, a.shape[1])
    grads = (by_owner(grad_gate), by_owner(grad_raw), by_owner(grad_output))
    width = error_left.shape[0]
    lefts = local_call(
        left_kernel, tall(group * width), me, start_in, start_out, *grads, error_left, scalars=1,
        name="left",
    )
    lefts = sum_everywhere(lefts, 1)
    vectors = tiles_of(small_total.shape[0] * 128 // 1024)
    flat = lambda a: jnp.pad(a, (0, vectors * 1024 - a.shape[0])).reshape(vectors, 8, 128)
    per_owner = -(-((PROJ + D) // 128 + vectors) // group)
    rights, own_left = local_call(
        partial(right_kernel, replicas),
        (tall(group * per_owner), tall(width)),
        me, lefts, *grads, input_error[0], output_error[0], flat(small_total),
        scalars=1,
        scratch=[pltpu.VMEM((group * width, 8, 128), F32)],
        name="right",
    )
    rights = sum_everywhere(rights, 2)
    new_input_weight, new_output_weight, new_input_momentum, new_output_momentum = local_call(
        partial(update_kernel, (rate_in, rate_out), replicas),
        tuple(map(like, (input_weight, output_weight, input_momentum, output_momentum))),
        rights, own_left, input_weight, output_weight, input_momentum, output_momentum,
        name="update",
    )
    new_input_error, new_output_error = local_call(
        partial(residual_kernel, replicas),
        (like(input_error[0]), like(output_error[0])),
        rights, own_left, gate_total, raw_total, output_total, input_error[0], output_error[0],
        name="residual",
    )
    rows_of = lambda tiles, amount: tiles.transpose(0, 2, 1).reshape(-1, 8)[:amount]
    ahead = tiles_of(input_weight.shape[0])
    input_left = rows_of(own_left[:ahead], input_weight.shape[0])
    output_left = rows_of(own_left[ahead:], output_weight.shape[0])
    input_right = rows_of(rights[: PROJ // 128], PROJ) / replicas
    output_right = rows_of(rights[PROJ // 128 : (PROJ + D) // 128], D) / replicas
    small_sum = rights[(PROJ + D) // 128 :].reshape(-1)[: small_values.shape[0]]
    new_small_momentum = MOMENTUM * small_momentum + small_sum / replicas
    new_small_values = small_values - rate_small * new_small_momentum
    return (
        output.reshape(shape),
        input_grad.reshape(shape),
        new_input_weight,
        new_output_weight,
        new_input_momentum,
        new_output_momentum,
        new_small_values,
        new_small_momentum,
        input_left,
        input_right,
        output_left,
        output_right,
        new_input_error[None],
        new_output_error[None],
    )


def solution(mesh):
    return jax.shard_map(
        body,
        mesh=mesh,
        in_specs=(
            P(None, ("rep", "fsdp"), "seq", None),
            P(None, ("rep", "fsdp"), "seq", None),
            P(None, ("rep", "fsdp"), None),
            P(("fsdp", "seq"), None),
            P(("fsdp", "seq"), None),
            P(),
            P(("fsdp", "seq"), None),
            P(("fsdp", "seq"), None),
            P(),
            P("rep", ("fsdp", "seq"), None),
            P("rep", ("fsdp", "seq"), None),
            P(),
            P(),
        ),
        out_specs=(
            P(None, ("rep", "fsdp"), "seq", None),
            P(None, ("rep", "fsdp"), "seq", None),
            P(("fsdp", "seq"), None),
            P(("fsdp", "seq"), None),
            P(("fsdp", "seq"), None),
            P(("fsdp", "seq"), None),
            P(),
            P(),
            P(("fsdp", "seq"), None),
            P(),
            P(("fsdp", "seq"), None),
            P(),
            P("rep", ("fsdp", "seq"), None),
            P("rep", ("fsdp", "seq"), None),
        ),
        check_vma=False,
    )
```

time: 1130 us -> 329 us (0.29)
  local copies, waits for them, and re-layouts: 313 us -> 34.2 us
  matrix products: 278 us -> 31.8 us
  other arithmetic: 223 us -> 18.5 us
  Pallas kernels: 0 us -> 180 us
  waiting for transfers between devices: 185 us -> 41 us
  blocking collectives: 82.4 us -> 0 us
  loops' own time: 14.4 us -> 0 us
    dot_general x82 -> x8, matrix products: 277 us -> 31.8 us  [the longest x1 6.92 us: body(): jnp.einsum('nkl,dk->nld', ggate, gate_full, preferred_element_type=F32)]
    pallas_call x0 -> x11, Pallas kernels: none -> 180 us  [the longest x1 38.6 us: leave(): pl.pallas_call(leave_kernel, grid_spec=pltpu.PrefetchScalarGridSpec(num_s...]
    psum x1 -> x0, waiting for transfers between devices: 122 us -> none  [body(): lax.psum((jnp.dot(input_mixed.T, input_left, precision=HIGH), jnp.dot(out...]
    another operation x178 -> x16, local copies, waits for them, and re-layouts: 85.7 us -> 10.9 us  [the longest x6 7.66 us: body(): jnp.stack([jnp.where(ahead[:, j:j + length + 8] == ahead[:, :length + 8],...]
    psum x3 -> x0, blocking collectives: 68.6 us -> none  [the longest x1 37.2 us: body(): lax.psum((jnp.dot(input_mixed.T, input_left, precision=HIGH), jnp.dot(out...]
    squeeze x57 -> x0, local copies, waits for them, and re-layouts: 50 us -> none  [the longest x40 29.7 us: run_states(): lax.scan(jax.checkpoint(advance), beginning, current_all)]
    another operation x71 -> x5, other arithmetic: 51.9 us -> 3.28 us
    reduce_sum x20 -> x4, other arithmetic: 38.6 us -> 2.95 us  [the longest x2 1.95 us: body(): jnp.sum((outgoing.astype(F32) * send.astype(F32)).reshape(pieces, HEADS,...]
  transfers between devices with their start and end apart: 9 -> 10, of which waited for: 5 -> 3; matrix products, arithmetic and copies ran while one was open for 52% -> 23% of each run, Pallas kernels for 0% -> 42%
where the time goes in v1:
time: 329 us; the launch traced here: 328 us
  Pallas kernels  180 us (55%)
  waiting for transfers between devices  41 us (12%)
  local copies, waits for them, and re-layouts  34.2 us (10%)
  matrix products  31.8 us (10%)
  other arithmetic  18.5 us (6%)
  between operations  14.7 us (4%)
  starting transfers between devices  7.78 us (2%)
    pallas_call x1, Pallas kernels, leave(): pl.pallas_call(leave_kernel, grid_spec=pltpu.PrefetchScalarGridSpec(num_s...  38.6 us
    pallas_call x2, Pallas kernels, sum_everywhere(): pl.pallas_call(partial(sum_kernel, width, group, replicas), out_shape=jax...  36.9 us
    all_gather x3, waiting for transfers between devices, gather_rows(): return lax.all_gather(shard, ('fsdp', 'seq'), axis=0, tiled=True)  36.7 us
    pallas_call x4, Pallas kernels, local_call(): pl.pallas_call(kernel, out_shape=outs, in_specs=[pl.BlockSpec(memory_spac...  24.9 us
    pallas_call x1, Pallas kernels, enter(): pl.pallas_call(enter_kernel, grid=(n,), in_specs=[one(length, D), one(HAL...  23.9 us
    pallas_call x1, Pallas kernels, backward_scan(): pl.pallas_call(backward_kernel, grid_spec=pltpu.PrefetchScalarGridSpec(nu...  20.8 us
    pallas_call x1, Pallas kernels, conv_back(): pl.pallas_call(conv_back_kernel, grid=(tiles, n), in_specs=[pl.BlockSpec(...  20.7 us
    pallas_call x1, Pallas kernels, forward_scan(): pl.pallas_call(forward_kernel, grid_spec=pltpu.PrefetchScalarGridSpec(num...  13.9 us
  transfers between devices with their start and end apart: 10, of which 3 were waited for; matrix products, arithmetic and copies ran while one was open for 23% of the time, Pallas kernels for 42%

profile of v1, /device:TPU:0, one launch (start us, length us, event | category | flops | bytes accessed | tf_op | source)
XLA Modules:
  0.0 327.7 jit_solution(9376184954624431200)
XLA Ops:
  7.3 1.5 convert.10
  12.1 2.3 collective-permute-start
  23.2 1.6 stack.57.same_ref
  24.8 19.2 %all-gather.4.cloned.1.call-done.wraw_ref = bf16[768,1792]{1,0:T(8,128)(2,1)} async-done(((bf16[96,1792]{1,0:T(8,128)(2,1)}), bf16[768,1792]{1,0:T(8,128)(2,1)}) %all-gather.4.cloned.1.call-update) | async-done | bytes 2752528 | tf_op jit(solution)/shard_map/all_gather | solution.py:922
  44.0 23.9 %enter.1 = (bf16[2,512,768]{2,1,0:T(8,128)(2,1)}, bf16[2,528,1792]{2,1,0:T(8,128)(2,1)}, bf16[2,512,1792]{2,1,0:T(8,128)(2,1)}, bf16[2,1536,512]{2,1,0:T(8,128)(...) custom-call(bf16[2,512,768]{2,1,0:T(8,128)(2,1)} %bitcast.134, ...), custom_call_target="tpu_custom_call" | custom-call | tf_op jit(solution)/shard_map/enter/pallas_call | solution.py:149
  67.9 2.4 collective-permute-start.1
  75.6 13.9 %forward_scan.1 = (f32[2,1536,512]{2,1,0:T(8,128)}, bf16[2,4,1536,128]{3,2,1,0:T(8,128)(2,1)}) custom-call(s32[2,4,3]{2,1,0:T(4,128)} %pad_add_fusion.marks_ref, bf16[2,1536,512]{2,1,0:T(8,128)(2,1)} %get-tuple-element.50.val_ref, bf16[2,512,256]{2,1,0:T(8,128)(2,1)} %get-tuple-element.51.w_ref.r_ref, bf16[2,512,256]{2,1,0:T(8,128)(2,1)} %get-tuple-element.51.w_ref.r_ref, ...), custom_call_target="tpu_custom_call" | custom-call | tf_op jit(solution)/shard_map/forward_scan/pallas_call | solution.py:221
  89.5 17.6 %all-gather.8.cloned.1.call-done.wout_ref = bf16[1536,768]{1,0:T(8,128)(2,1)} async-done(((bf16[192,768]{1,0:T(8,128)(2,1)}), bf16[1536,768]{1,0:T(8,128)(2,1)}) %all-gather.8.cloned.1.call-update) | async-done | bytes 2359312 | tf_op jit(solution)/shard_map/all_gather | solution.py:922
  107.0 38.6 %leave.1 = (bf16[2,512,768]{2,1,0:T(8,128)(2,1)}, bf16[2,1536,512]{2,1,0:T(8,128)(2,1)}, bf16[2,1536,512]{2,1,0:T(8,128)(2,1)}, f32[2,32,512]{2,1,0:T(8,128)}, b...) custom-call(s32[2,4,3]{2,1,0:T(4,128)} %pad_add_fusion.marks_ref, ...), custom_call_target="tpu_custom_call" | custom-call | tf_op jit(solution)/shard_map/leave/pallas_call | solution.py:513
  145.7 5.9 %bitcast_convert_fusion.1 = bf16[768,1536]{1,0:T(8,128)(2,1)} fusion(bf16[2,512,768]{2,1,0:T(8,128)(2,1)S(1)} %copy-done.3, bf16[2,1536,512]{2,1,0:T(8,128)(2,1)} %get-tuple-element.56), kind=kOutput, calls=%fused_computation.5 | convolution fusion | flops 2417098752 | bytes 7077888 | tf_op jit(solution)/shard_map/nld,nkl->dk/dot_general | solution.py:1021
  161.7 2.9 stack.63.near_ref
  164.9 6.9 %fusion.9 = f32[2,512,768]{2,1,0:T(8,128)} fusion(bf16[2,1536,512]{2,1,0:T(8,128)(2,1)} %get-tuple-element.56, bf16[768,1536]{1,0:T(8,128)(2,1)} %all-gather.6.cloned.1.call-done.wgate_ref), kind=kOutput, calls=%fused_computation.16 | convolution fusion | flops 2415919104 | bytes 8650752 | tf_op jit(solution)/shard_map/nkl,dk->nld/dot_general | solution.py:1040
  171.9 2.0 reduce.3
  174.5 1.9 multiply_reduce_fusion
  177.3 20.8 %backward_scan.1 = (bf16[2,1536,512]{2,1,0:T(8,128)(2,1)}, f32[2,512,256]{2,1,0:T(8,128)}, f32[2,32,512]{2,1,0:T(8,128)}, f32[32,1]{1,0:T(8,128)}, f32[32,1]{1,0:T(8,128)}) custom-call(s32[2,4,3]{2,1,0:T(4,128)} %pad_add_fusion.marks_ref, bf16[2,1536,512]{2,1,0:T(8,128)(2,1)} %get-tuple-element.50.val_ref, ...), custom_call_target="tpu_custom_call" | custom-call | tf_op jit(solution)/shard_map/backward_scan/pallas_call | solution.py:339
  198.1 20.7 %conv_back.1 = (bf16[2,512,1792]{2,1,0:T(8,128)(2,1)}, f32[2,16,1792]{2,1,0:T(8,128)}, f32[2,8,1792]{2,1,0:T(8,128)}, f32[8,1792]{1,0:T(8,128)}) custom-call(bf16[2,1536,512]{2,1,0:T(8,128)(2,1)} %get-tuple-element.62.gval_ref, f32[2,512,256]{2,1,0:T(8,128)} %get-tuple-element.63.gwr_ref, bf16[2,512,1792]{2,1,0:T(8,128)(2,1)} %get-tuple-element.64.dsilu_ref, ...), custom_call_target="tpu_custom_call" | custom-call | tf_op jit(solution)/shard_map/conv_back/pallas_call | solution.py:612
  220.1 1.4 convolution_bitcast_fusion
  222.7 1.4 slice.148
  224.1 1.4 reshape.133
  226.8 1.4 slice_reduce_fusion.3
  228.3 1.7 fusion.14
  230.0 6.4 %bitcast_convert_fusion = bf16[768,1792]{1,0:T(8,128)(2,1)} fusion(bf16[2,512,768]{2,1,0:T(8,128)(2,1)S(1)} %copy-done.3, bf16[2,512,1792]{2,1,0:T(8,128)(2,1)} %fusion.14), kind=kOutput, calls=%fused_computation | convolution fusion | flops 2819948544 | bytes 7995392 | tf_op jit(solution)/shard_map/nld,nlk->dk/dot_general | solution.py:1035
  236.4 6.2 %left.1.x_ref = f32[24,8,128]{2,1,0:T(8,128)} custom-call(s32[1]{0:T(128)} %bitcast.24.me_ref, bf16[24,3328]{1,0:T(8,128)(2,1)} %pad_maximum_fusion.sin_ref, bf16[24,768]{1,0:T(8,128)(2,1)} %pad_maximum_fusion.1.sout_ref, bf16[8,96,1536]{2,1,0:T(8,128)(2,1)} %bitcast.140, bf16[8,96,1792]{2,1,0:T(8,128)(2,1)} %bitcast.136, bf16[8,192,768]{2,1,0:T(8,128)(2,1)} %bitcast.138, ...), custom_call_target="tpu_custom_call" | custom-call | tf_op jit(solution)/shard_map/left/pallas_call | solution.py:871
  242.6 17.5 %sum_everywhere.2.left_ref = f32[24,8,128]{2,1,0:T(8,128)} custom-call(f32[24,8,128]{2,1,0:T(8,128)} %left.1.x_ref), custom_call_target="tpu_custom_call" | custom-call | tf_op jit(solution)/shard_map/sum_everywhere/pallas_call | solution.py:708
  260.1 6.1 %fusion.7 = f32[2,512,768]{2,1,0:T(8,128)S(1)} fusion(bf16[2,512,1792]{2,1,0:T(8,128)(2,1)} %fusion.14, bf16[768,1792]{1,0:T(8,128)(2,1)} %all-gather.4.cloned.1.call-done.wraw_ref), kind=kOutput, calls=%fused_computation.14 | convolution fusion | flops 2818572288 | bytes 9568256 | tf_op jit(solution)/shard_map/nlk,dk->nld/dot_general | solution.py:1041
  266.3 3.5 %fusion.6 = (f32[768]{0:T(1024)S(1)}, f32[2,512]{1,0:T(2,128)}, f32[2,512,768]{2,1,0:T(8,128)}) fusion(f32[2,512]{1,0:T(2,128)S(1)} %add_rsqrt_fusion, bf16[2,1,512,768]{3,2,1,0:T(8,128)(2,1)S(1)} %copy-done, f32[768]{0:T(1024)S(1)} %slice.129, bf16[768,24]{1,0:T(8,128)(2,1)S(1)} %convert_element_type.82, f32[2,32,512]{2,1,0:T(8,128)S(1)} %copy-done.12, ...), kind=kOutput, calls=%fused_computation.12 | convolution fusion | flops 44824832 | bytes 11271168 | tf_op jit(solution)/shard_map/nhl,dh->nld/dot_general | solution.py:1042
  270.5 9.1 %right.1 = (f32[64,8,128]{2,1,0:T(8,128)}, f32[3,8,128]{2,1,0:T(8,128)}) custom-call(s32[1]{0:T(128)} %bitcast.24.me_ref, f32[24,8,128]{2,1,0:T(8,128)} %sum_everywhere.2.left_ref, bf16[8,96,1536]{2,1,0:T(8,128)(2,1)} %bitcast.141, bf16[8,96,1792]{2,1,0:T(8,128)(2,1)} %bitcast.137, bf16[8,192,768]{2,1,0:T(8,128)(2,1)} %bitcast.139, f32[96,3328]{1,0:T(8,128)} %bitcast.142, ...), custom_call_target="tpu_custom_call" | custom-call | tf_op jit(solution)/shard_map/right/pallas_call | solution.py:871
  280.5 19.3 %sum_everywhere.3.x_ref = f32[64,8,128]{2,1,0:T(8,128)} custom-call(f32[64,8,128]{2,1,0:T(8,128)} %get-tuple-element.76.x_ref), custom_call_target="tpu_custom_call" | custom-call | tf_op jit(solution)/shard_map/sum_everywhere/pallas_call | solution.py:708
  299.8 5.3 %update.1 = (f32[96,3328]{1,0:T(8,128)}, f32[192,768]{1,0:T(8,128)}, f32[96,3328]{1,0:T(8,128)}, f32[192,768]{1,0:T(8,128)}) custom-call(f32[64,8,128]{2,1,0:T(8,128)} %sum_everywhere.3.x_ref, f32[3,8,128]{2,1,0:T(8,128)} %get-tuple-element.77.own_ref, f32[96,3328]{1,0:T(8,128)} %win_ref.1, f32[192,768]{1,0:T(8,128)} %wout_ref.1, f32[96,3328]{1,0:T(8,128)} %min_ref.1, ...), custom_call_target="tpu_custom_call" | custom-call | tf_op jit(solution)/shard_map/update/pallas_call | solution.py:871
  307.0 3.9 %fusion.11 = bf16[2,1,512,768]{3,2,1,0:T(8,128)(2,1)} fusion(f32[2,512,768]{2,1,0:T(8,128)} %get-tuple-element.200, f32[2,512]{1,0:T(2,128)S(1)} %fusion.20, f32[768]{0:T(1024)S(1)} %slice.129, f32[2,512]{1,0:T(2,128)S(1)} %add_rsqrt_fusion, bf16[2,1,512,768]{3,2,1,0:T(8,128)(2,1)S(1)} %copy-done.2, bf16[2,1,512,768]{3,2,1,0:T(8,128)(2,1)S(1)} %copy-done), kind=kLoop, calls=%fused_computation.18 | loop fusion | flops 6291456 | bytes 7875584
  312.3 4.2 %reduce-scatter.6.cloned.1.call-done.raw_ref = bf16[96,1792]{1,0:T(8,128)(2,1)} async-done(((bf16[768,1792]{1,0:T(8,128)(2,1)}), bf16[96,1792]{1,0:T(8,128)(2,1)}) %reduce-scatter.6.cloned.1.call-update) | async-done | bytes 344080 | tf_op jit(solution)/shard_map/reduce_scatter | solution.py:926
  316.5 4.3 %residual.1 = (f32[96,3328]{1,0:T(8,128)}, f32[192,768]{1,0:T(8,128)}) custom-call(f32[64,8,128]{2,1,0:T(8,128)} %sum_everywhere.3.x_ref, f32[3,8,128]{2,1,0:T(8,128)} %get-tuple-element.77.own_ref, bf16[96,1536]{1,0:T(8,128)(2,1)} %reduce-scatter.4.cloned.1.call-done.gate_ref, bf16[96,1792]{1,0:T(8,128)(2,1)} %reduce-scatter.6.cloned.1.call-done.raw_ref, ...), custom_call_target="tpu_custom_call" | custom-call | tf_op jit(solution)/shard_map/residual/pallas_call | solution.py:871
  (158 shorter events, 37.8 us)
Async XLA Ops:
  7.2 7.2 %copy-start.25 = (s32[2,1,1024]{2,1,0:T(1,128)S(1)}, s32[2,1,1024]{2,1,0:T(1,128)}, u32[]{:S(2)}) copy-start(s32[2,1,1024]{2,1,0:T(1,128)} %param.15) | copy-start | bytes 24580
  7.2 7.2 %copy-start.10 = (f32[29768]{0:T(1024)S(1)}, f32[29768]{0:T(1024)}, u32[]{:S(2)}) copy-start(f32[29768]{0:T(1024)} %param.18) | copy-start | bytes 357220
  7.2 7.6 %copy-start.8 = (f32[3328,8]{0,1:T(8,128)S(1)}, f32[3328,8]{0,1:T(8,128)}, u32[]{:S(2)}) copy-start(f32[3328,8]{0,1:T(8,128)} %param.24) | copy-start | bytes 319492
  7.2 7.6 %copy-start.1 = (f32[1,96,3328]{2,1,0:T(8,128)S(1)}, f32[1,96,3328]{2,1,0:T(8,128)}, u32[]{:S(2)}) copy-start(f32[1,96,3328]{2,1,0:T(8,128)} %param.22) | copy-start | bytes 3833860
  7.2 36.7 %all-gather.4.cloned.1.call-start = ((), (), s32[]{:S(2)}) async-start(), calls=%async_computation.3 | async-start | bytes 3096576 | tf_op jit(solution)/shard_map/all_gather | solution.py:922
  9.6 79.9 %all-gather.6.cloned.1.call-start = ((), (), s32[]{:S(2)}) async-start(), calls=%async_computation.4 | async-start | bytes 2654208 | tf_op jit(solution)/shard_map/all_gather | solution.py:922
  10.4 96.6 %all-gather.8.cloned.1.call-start = ((), (), s32[]{:S(2)}) async-start(), calls=%async_computation.5 | async-start | bytes 2654208 | tf_op jit(solution)/shard_map/all_gather | solution.py:922
  11.2 301.1 %reduce-scatter.4.cloned.1.call-start = ((), (), s32[]{:S(2)}) async-start(), calls=%async_computation.6 | async-start | bytes 2654208 | tf_op jit(solution)/shard_map/reduce_scatter | solution.py:926
  12.1 12.7 %collective-permute-start = (bf16[2,16,768]{2,1,0:T(8,128)(2,1)S(1)}, bf16[2,16,768]{2,1,0:T(8,128)(2,1)S(1)}, u32[]{:S(2)}, u32[]{:S(2)}) collective-permute-start(bf16[2,16,768]{2,1,0:T(8,128)(2,1)S(1)} %slice.162), channel_id=1, source_target_pairs={{0,1},{2,3},{4,5},{6,7},{8,9},{10,11},{12,13},{14,15},{16,17},{18,... | collective-permute-start | bytes 147464 | tf_op jit(solution)/shard_map/ppermute | solution.py:910
  24.8 49.3 %copy-start.4 = (f32[1,192,768]{2,1,0:T(8,128)S(1)}, f32[1,192,768]{2,1,0:T(8,128)}, u32[]{:S(2)}) copy-start(f32[1,192,768]{2,1,0:T(8,128)} %param.23) | copy-start | bytes 1769476
  24.8 49.3 %copy-start.13 = (f32[768,8]{0,1:T(8,128)S(1)}, f32[768,8]{0,1:T(8,128)}, u32[]{:S(2)}) copy-start(f32[768,8]{0,1:T(8,128)} %param.25) | copy-start | bytes 73732
  24.8 19.2 %copy-start.17 = (bf16[2,16,768]{2,1,0:T(8,128)(2,1)}, bf16[2,16,768]{2,1,0:T(8,128)(2,1)S(1)}, u32[]{:S(2)}) copy-start(bf16[2,16,768]{2,1,0:T(8,128)(2,1)S(1)} %collective-permute-done.halo_ref) | copy-start | bytes 147460
  67.9 6.8 %collective-permute-start.1 = (bf16[2,1536,128]{2,1,0:T(8,128)(2,1)}, bf16[2,1536,128]{2,1,0:T(8,128)(2,1)S(1)}, u32[]{:S(2)}, u32[]{:S(2)}) collective-permute-start(bf16[2,1536,128]{2,1,0:T(8,128)(2,1)} %get-tuple-element.53), channel_id=1, source_target_pairs={{0,1},{2,3},{4,5},{6,7},{8,9},{10,11},{12,13},{14,15},{16,17},{18,... | collective-permute-start | bytes 2359304 | tf_op jit(solution)/shard_map/ppermute | solution.py:910
  107.0 38.7 %copy-start.3 = (bf16[2,512,768]{2,1,0:T(8,128)(2,1)S(1)}, bf16[2,512,768]{2,1,0:T(8,128)(2,1)}, u32[]{:S(2)}) copy-start(bf16[2,512,768]{2,1,0:T(8,128)(2,1)} %get-tuple-element.49.normed_ref) | copy-start | bytes 4718596
  151.6 4.8 %copy-start.23 = (f32[1,8,128]{2,1,0:T(8,128)S(1)}, f32[1,8,128]{2,1,0:T(8,128)}, u32[]{:S(2)}) copy-start(f32[1,8,128]{2,1,0:T(8,128)} %pad_bitcast_fusion.2) | copy-start | bytes 12292
  151.6 160.7 %reduce-scatter.8.cloned.1.call-start = ((), (), s32[]{:S(2)}) async-start(), calls=%async_computation.8 | async-start | bytes 2654208 | tf_op jit(solution)/shard_map/reduce_scatter | solution.py:926
  153.4 11.2 %copy-start.18 = (f32[2,512]{1,0:T(2,128)}, f32[2,512]{1,0:T(2,128)S(1)}, u32[]{:S(2)}) copy-start(f32[2,512]{1,0:T(2,128)S(1)} %fusion) | copy-start | bytes 12292
  155.1 19.4 %collective-permute-start.2 = (bf16[2,1536,128]{2,1,0:T(8,128)(2,1)}, bf16[2,1536,128]{2,1,0:T(8,128)(2,1)}, u32[]{:S(2)}, u32[]{:S(2)}) collective-permute-start(bf16[2,1536,128]{2,1,0:T(8,128)(2,1)} %get-tuple-element.61), channel_id=1, source_target_pairs={{1,0},{3,2},{5,4},{7,6},{9,8},{11,10},{13,12},{15,14},{17,16},{19,... | collective-permute-start | bytes 2359304 | tf_op jit(solution)/shard_map/ppermute | solution.py:914
  164.7 9.2 %copy-start.24 = (f32[32,128]{1,0:T(8,128)S(1)}, f32[32,128]{1,0:T(8,128)}, u32[]{:S(2)}) copy-start(f32[32,128]{1,0:T(8,128)} %get-tuple-element.75) | copy-start | bytes 49156
  164.7 151.9 %reduce-scatter.6.cloned.1.call-start = ((), (), s32[]{:S(2)}) async-start(), calls=%async_computation.7 | async-start | bytes 3096576 | tf_op jit(solution)/shard_map/reduce_scatter | solution.py:926
  198.1 22.0 %copy-start.12 = (f32[2,32,512]{2,1,0:T(8,128)S(1)}, f32[2,32,512]{2,1,0:T(8,128)}, u32[]{:S(2)}) copy-start(f32[2,32,512]{2,1,0:T(8,128)} %get-tuple-element.69) | copy-start | bytes 393220
  218.8 9.5 %collective-permute-start.3 = (f32[2,8,1792]{2,1,0:T(8,128)}, f32[2,8,1792]{2,1,0:T(8,128)}, u32[]{:S(2)}, u32[]{:S(2)}) collective-permute-start(f32[2,8,1792]{2,1,0:T(8,128)} %get-tuple-element.68), channel_id=1, source_target_pairs={{1,0},{3,2},{5,4},{7,6},{9,8},{11,10},{13,12},{15,14},{17,16},{19,... | collective-permute-start | bytes 344072 | tf_op jit(solution)/shard_map/ppermute | solution.py:914
  260.1 6.1 %copy-start.6 = (f32[2,512,768]{2,1,0:T(8,128)S(1)}, f32[2,512,768]{2,1,0:T(8,128)}, u32[]{:S(2)}) copy-start(f32[2,512,768]{2,1,0:T(8,128)} %fusion.9) | copy-start | bytes 9437188
  266.2 3.5 %copy-start.15 = (f32[7168]{0:T(1024)S(1)}, f32[7168]{0:T(1024)}, u32[]{:S(2)}) copy-start(f32[7168]{0:T(1024)} %reshape.133) | copy-start | bytes 86020
  266.2 3.5 %copy-start.20 = (f32[1536]{0:T(1024)S(1)}, f32[1536]{0:T(1024)}, u32[]{:S(2)}) copy-start(f32[1536]{0:T(1024)} %reduce.3) | copy-start | bytes 18436
  279.7 26.1 %copy-start.19 = (f32[2,512]{1,0:T(2,128)S(1)}, f32[2,512]{1,0:T(2,128)}, u32[]{:S(2)}) copy-start(f32[2,512]{1,0:T(2,128)} %copy-done.18) | copy-start | bytes 12292
  279.7 26.1 %copy-start.22 = (f32[2,512]{1,0:T(2,128)S(1)}, f32[2,512]{1,0:T(2,128)}, u32[]{:S(2)}) copy-start(f32[2,512]{1,0:T(2,128)} %get-tuple-element.183) | copy-start | bytes 12292
  279.7 26.1 %copy-start.16 = (f32[3,8,128]{2,1,0:T(8,128)S(1)}, f32[3,8,128]{2,1,0:T(8,128)}, u32[]{:S(2)}) copy-start(f32[3,8,128]{2,1,0:T(8,128)} %get-tuple-element.77.own_ref) | copy-start | bytes 36868
  279.7 27.3 %copy-start.2 = (bf16[2,1,512,768]{3,2,1,0:T(8,128)(2,1)S(1)}, bf16[2,1,512,768]{3,2,1,0:T(8,128)(2,1)}, u32[]{:S(2)}) copy-start(bf16[2,1,512,768]{3,2,1,0:T(8,128)(2,1)} %param.14) | copy-start | bytes 4718596
  299.8 6.6 %copy-start.5 = (f32[64,8,128]{2,1,0:T(8,128)S(1)}, f32[64,8,128]{2,1,0:T(8,128)}, u32[]{:S(2)}) copy-start(f32[64,8,128]{2,1,0:T(8,128)} %sum_everywhere.3.x_ref) | copy-start | bytes 786436
  307.0 4.6 %copy-start.11 = (f32[29768]{0:T(1024)S(1)}, f32[29768]{0:T(1024)}, u32[]{:S(2)}) copy-start(f32[29768]{0:T(1024)} %param.18) | copy-start | bytes 357220
  307.0 4.6 %copy-start.14 = (f32[29768]{0:T(1024)S(1)}, f32[29768]{0:T(1024)}, u32[]{:S(2)}) copy-start(f32[29768]{0:T(1024)} %param.21) | copy-start | bytes 357220
  (7 other events, 19.6 us)
Sparse Core Ops, SparseCore 0:
  10.5 33.4 all-gather.3
  46.4 29.0 all-gather.5
  77.9 29.0 all-gather.7
  151.7 43.3 reduce-scatter.3
  198.7 42.4 reduce-scatter.7
  270.7 45.8 reduce-scatter.5
